TPU v7x, 128 devices: a whole 4x4x4 slice. The times are simulated.
128 devices in a mesh: section: 2 (over z_hi), dp: 4 (over z_lo, core), seq: 16 (over x, y).
Axes of the slice: x: 4, y: 4, z: 4 (z_hi: 2, z_lo: 2; z = z_hi * 2 + z_lo), core: 2. Of those that a mesh axis runs over, the one named last changes fastest.
Arguments:
- enc_states: bfloat16 [8, 2048, 4096], P(('section', 'dp'), 'seq'), may hold values from -6 to 6
- enc_gain: float32 [4096], replicated, may hold values from 0.1 to 1.9
- key_weight: bfloat16 [4096, 4096], P(None, 'seq'), may hold values from -0.09375 to 0.09375
- value_weight: bfloat16 [4096, 4096], P(None, 'seq'), may hold values from -0.09375 to 0.09375
- queries: bfloat16 [8, 512, 4096], P(('section', 'dp'), None, 'seq'), may hold values from -28 to 28
- out_grad: bfloat16 [8, 512, 4096], P(('section', 'dp'), None, 'seq'), may hold values from -6 to 6
- lengths: int32 [8], replicated, may hold values from 1024 to 2048, as said below
Outputs:
- attended: bfloat16 [8, 512, 4096], P(('section', 'dp'), None, 'seq')
- enc_grad: bfloat16 [8, 2048, 4096], P(('section', 'dp'), 'seq')
- key_grad: float32 [4096, 4096], P(('section', 'dp'), 'seq')
- value_grad: float32 [4096, 4096], P(('section', 'dp'), 'seq')
- query_grad: bfloat16 [8, 512, 4096], P(('section', 'dp'), None, 'seq')
Inputs may be any that keep to these rules, and one draw needn't show every extreme that they name: `lengths`: positions at or beyond a sequence's length are padding; at least one sequence in every draw has length 2048.
All inputs are finite; a program needn't handle non-finite values.
Results may differ from a plain program's by a relative error of at most 0.023.
The roundings to bfloat16 on the way count: a program that leaves them out, or rounds other values in their place, can miss the bound.
Values may be sent and summed in bfloat16 or wider, within the bound.
A program may use at most 128 MiB of HBM per device.

v0:
```python
import jax
import jax.numpy as jnp
from jax import lax
from jax.sharding import PartitionSpec as P

HD = 256


EPS = 1e-06
NEG_FILL = -1e30


def partner_2(value, axis, stride):
    mask = 2**stride
    pairs = [(source, source ^ mask) for source in range(lax.axis_size(axis))]
    return lax.ppermute(value, axis, pairs)


def normalize(enc_rows, gain):
    wide_rows = enc_rows.astype(jnp.float32)
    factor = lax.rsqrt(jnp.mean(wide_rows * wide_rows, axis=-1, keepdims=True) + EPS)
    return ((wide_rows * factor * gain).astype(jnp.bfloat16), factor)


def norm_backward(enc_rows, factor, gain, row_grad):
    wide_rows = enc_rows.astype(jnp.float32)
    scaled = row_grad.astype(jnp.float32) * gain
    inner_sum = jnp.mean(scaled * wide_rows, axis=-1, keepdims=True)
    return (factor * scaled - wide_rows * factor * factor * factor * inner_sum).astype(jnp.bfloat16)


def attend(query_rows, key_rows, value_rows, upstream, visible):
    score_scale = HD ** (-0.5)
    scores = (
        jnp.einsum("thd,shd->hts", query_rows, key_rows, preferred_element_type=jnp.float32)
        * score_scale
    )
    scores = jnp.where(visible[None, None, :], scores, NEG_FILL)
    row_max = jnp.max(scores, axis=-1, keepdims=True)
    exponent = jnp.exp(scores - row_max)
    probability = exponent / jnp.sum(exponent, axis=-1, keepdims=True)
    prob_weights = probability.astype(jnp.bfloat16)
    attended = jnp.einsum(
        "hts,shd->thd", prob_weights, value_rows, preferred_element_type=jnp.float32
    ).astype(jnp.bfloat16)
    grad_probs = jnp.einsum(
        "thd,shd->hts", upstream, value_rows, preferred_element_type=jnp.float32
    )
    inner_sum = jnp.sum(probability * grad_probs, axis=-1, keepdims=True)
    grad_scores = (probability * (grad_probs - inner_sum) * score_scale).astype(jnp.bfloat16)
    query_grad = jnp.einsum(
        "hts,shd->thd", grad_scores, key_rows, preferred_element_type=jnp.float32
    ).astype(jnp.bfloat16)
    key_grad = jnp.einsum(
        "hts,thd->shd", grad_scores, query_rows, preferred_element_type=jnp.float32
    ).astype(jnp.bfloat16)
    value_grad = jnp.einsum(
        "hts,thd->shd", prob_weights, upstream, preferred_element_type=jnp.float32
    ).astype(jnp.bfloat16)
    return (attended, query_grad, key_grad, value_grad)


def on_device(enc_states, enc_gain, key_weight, value_weight, queries, out_grad, lengths):
    enc_rows = enc_states[0]
    normed, factor = normalize(enc_rows, enc_gain)
    head_width = key_weight.shape[1]
    heads_here = head_width // HD
    projection = jnp.concatenate([key_weight, value_weight], axis=1)
    dp_count = lax.axis_size("dp")
    batch_count = lax.axis_size("section") * dp_count
    position = lax.axis_index("section") * dp_count + lax.axis_index("dp")
    partner = (position + dp_count) % batch_count
    src_rows = enc_rows.shape[0] * lax.axis_size("seq")
    positions = jnp.arange(src_rows, dtype=jnp.int32)
    target_rows = queries.shape[1]
    visible = positions < lengths[partner]
    partner_rows = partner_2(normed, "section", 0)
    gathered = lax.all_gather(partner_rows, "seq", axis=0, tiled=True)
    keys_values = jnp.dot(gathered, projection, preferred_element_type=jnp.float32).astype(
        jnp.bfloat16
    )
    query_rows = queries[0].reshape(target_rows, heads_here, HD)
    upstream = out_grad[0].reshape(target_rows, heads_here, HD)
    key_rows = keys_values[:, :head_width].reshape(src_rows, heads_here, HD)
    value_rows = keys_values[:, head_width:].reshape(src_rows, heads_here, HD)
    attended, query_grad, key_grad, value_grad = attend(
        query_rows, key_rows, value_rows, upstream, visible
    )
    kv_grads = jnp.concatenate(
        [key_grad.reshape(src_rows, head_width), value_grad.reshape(src_rows, head_width)], axis=1
    )
    attended, query_grad, kv_grads = (
        attended.reshape(target_rows, head_width),
        query_grad.reshape(target_rows, head_width),
        kv_grads,
    )
    row_share = lax.psum_scatter(
        lax.dot_general(
            kv_grads, projection, (((1,), (1,)), ((), ())), preferred_element_type=jnp.float32
        ).astype(jnp.bfloat16),
        "seq",
        scatter_dimension=0,
        tiled=True,
    )
    row_grad = partner_2(row_share, "section", 0)
    weight_term = lax.dot_general(
        gathered, kv_grads, (((0,), (0,)), ((), ())), preferred_element_type=jnp.float32
    )
    summed = lax.psum_scatter(
        weight_term.astype(jnp.bfloat16), ("section", "dp"), scatter_dimension=0, tiled=True
    ).astype(jnp.float32)
    enc_grad = norm_backward(enc_rows, factor, enc_gain, row_grad)
    return (
        attended[None],
        enc_grad[None],
        summed[:, :head_width],
        summed[:, head_width:],
        query_grad[None],
    )


def solution(mesh):
    placed = (
        P(("section", "dp"), "seq", None),
        P(),
        P(None, "seq"),
        P(None, "seq"),
        P(("section", "dp"), None, "seq"),
        P(("section", "dp"), None, "seq"),
        P(),
    )
    return jax.shard_map(
        on_device,
        mesh=mesh,
        in_specs=placed,
        out_specs=(
            P(("section", "dp"), None, "seq"),
            P(("section", "dp"), "seq", None),
            P(("section", "dp"), "seq"),
            P(("section", "dp"), "seq"),
            P(("section", "dp"), None, "seq"),
        ),
        check_vma=False,
    )
```

profile of v0, /device:TPU:1, one launch (start us, length us, event | category | flops | bytes accessed | tf_op | source)
XLA Modules:
  0.0 362.1 jit_solution(14198468222619220918)
XLA Ops:
  7.2 0.0 copy-start
  7.2 0.0 copy-start.10
  7.2 0.0 copy-start.4
  7.2 0.0 all-gather.2.cloned.1.call-start
  7.2 1.7 fusion.14
  8.9 1.6 fusion.9
  10.5 4.5 %collective-permute-start = (bf16[128,4096]{1,0:T(8,128)(2,1)S(1)}, bf16[128,4096]{1,0:T(8,128)(2,1)S(1)}, u32[]{:S(2)}, u32[]{:S(2)}) collective-permute-start(bf16[128,4096]{1,0:T(8,128)(2,1)S(1)} %fusion.9), channel_id=1, source_target_pairs={{0,64},{64,0},{1,65},{65,1},{2,66},{66,2},{3,67},{67,3},{4,68},{68... | collective-permute-start | bytes 3145736 | tf_op jit(solution)/shard_map/ppermute | solution.py:16
  15.0 22.9 %collective-permute-done = bf16[128,4096]{1,0:T(8,128)(2,1)S(1)} collective-permute-done((bf16[128,4096]{1,0:T(8,128)(2,1)S(1)}, bf16[128,4096]{1,0:T(8,128)(2,1)S(1)}, u32[]{:S(2)}, u32[]{:S(2)}) %collective-permute-start) | collective-permute-done | bytes 1048608 | tf_op jit(solution)/shard_map/ppermute | solution.py:16
  37.9 1.0 copy-done.6
  38.9 0.0 all-gather.2.cloned.1.call-update
  38.9 0.0 reduce-scatter.3.cloned.1.call-start
  38.9 0.0 copy-done.10
  39.0 0.0 copy-start.5
  39.0 0.6 dynamic_slice.3
  39.6 0.7 iota_compare_fusion
  40.2 0.0 copy-done.4
  40.3 1.5 constant_dynamic-update-slice_fusion.1
  41.8 0.0 copy-done.5
  41.8 1.5 constant_dynamic-update-slice_fusion
  43.3 109.2 %all-gather.2.cloned.1.call-done = bf16[2048,4096]{1,0:T(8,128)(2,1)} async-done(((bf16[128,4096]{1,0:T(8,128)(2,1)}), bf16[2048,4096]{1,0:T(8,128)(2,1)}) %all-gather.2.cloned.1.call-update) | async-done | bytes 16777232 | tf_op jit(solution)/shard_map/all_gather | solution.py:78
  152.5 13.6 %convolution_convert_fusion.2 = bf16[2048,512]{1,0:T(8,128)(2,1)S(1)} fusion(bf16[2048,4096]{1,0:T(8,128)(2,1)} %all-gather.2.cloned.1.call-done, bf16[4096,512]{1,0:T(8,128)(2,1)} %constant_dynamic-update-slice_fusion), kind=kOutput, calls=%fused_computation.17 | convolution fusion | flops 8590983168 | bytes 23068672 | tf_op jit(solution)/shard_map/dot_general | solution.py:79
  166.1 1.7 fusion.4
  167.8 0.0 copy-start.3
  167.8 1.0 fusion.5
  168.8 1.8 convolution_convert_fusion.3
  170.6 0.0 copy-start.12
  170.6 1.3 fusion
  172.0 0.0 copy-start.8
  172.0 1.5 fusion.3
  173.5 0.8 convolution_convert_fusion.4
  174.3 14.6 %convolution_convert_fusion = bf16[2048,4096]{1,0:T(8,128)(2,1)} fusion(bf16[4096,512]{1,0:T(8,128)(2,1)} %constant_dynamic-update-slice_fusion, bf16[2048,256]{0,1:T(8,128)(2,1)S(1)} %convolution_convert_fusion.3, bf16[2048,256]{0,1:T(8,128)(2,1)S(1)} %convolution_convert_fusion.4), kind=kOutput, calls=%fused_computation | convolution fusion | flops 8602517504 | bytes 23068672 | tf_op jit(solution)/shard_map/dot_general | solution.py:98
  188.9 0.0 reduce-scatter.3.cloned.1.call-update
  188.9 0.0 reduce-scatter.5.cloned.1.call-start
  188.9 14.3 %convolution_convert_fusion.1 = bf16[4096,512]{1,0:T(8,128)(2,1)} fusion(bf16[2048,4096]{1,0:T(8,128)(2,1)} %all-gather.2.cloned.1.call-done, bf16[2048,256]{0,1:T(8,128)(2,1)} %copy-done.12, bf16[2048,256]{0,1:T(8,128)(2,1)S(1)} %convolution_convert_fusion.4), kind=kOutput, calls=%fused_computation.1 | convolution fusion | flops 8596226048 | bytes 23068672 | tf_op jit(solution)/shard_map/dot_general | solution.py:106
  203.2 0.0 reduce-scatter.5.cloned.1.call-update
  203.3 95.6 %reduce-scatter.3.cloned.1.call-done = bf16[128,4096]{1,0:T(8,128)(2,1)} async-done(((bf16[2048,4096]{1,0:T(8,128)(2,1)}), bf16[128,4096]{1,0:T(8,128)(2,1)}) %reduce-scatter.3.cloned.1.call-update) | async-done | bytes 1048592 | tf_op jit(solution)/shard_map/reduce_scatter | solution.py:97
  298.9 2.8 collective-permute-start.1
  301.7 4.0 %fusion.16 = bf16[1,512,256]{1,2,0:T(8,128)(2,1)S(1)} fusion(bf16[2048,512]{1,0:T(8,128)(2,1)} %copy-done.11, f32[2048,512]{1,0:T(8,128)} %copy-done.3, f32[512]{0:T(512)S(1)} %fusion.5, f32[512]{0:T(512)S(1)} %get-tuple-element.12, pred[2048]{0:T(1024)(128)(4,1)S(1)} %iota_compare_fusion), kind=kOutput, calls=%fused_computation.33 | convolution fusion | flops 542244864 | bytes 5511168 | tf_op jit(solution)/shard_map/hts,shd->thd/dot_general | solution.py:43
  305.6 0.0 copy-start.2
  305.7 0.0 copy-start.9
  305.7 0.8 copy.12
  306.5 2.7 fusion.17
  309.2 1.8 copy.13
  311.0 37.9 %reduce-scatter.5.cloned.1.call-done = bf16[512,512]{1,0:T(8,128)(2,1)} async-done(((bf16[4096,512]{1,0:T(8,128)(2,1)}), bf16[512,512]{1,0:T(8,128)(2,1)}) %reduce-scatter.5.cloned.1.call-update) | async-done | bytes 524304 | tf_op jit(solution)/shard_map/reduce_scatter | solution.py:109
  348.9 2.1 fusion.33
  351.0 0.0 collective-permute-done.1
  351.0 1.6 fusion.15
  352.6 2.9 fusion.18
  (15 shorter events, 0.0 us)
Async XLA Ops:
  7.2 161.7 %copy-start = (bf16[1,512,256]{2,1,0:T(8,128)(2,1)S(1)}, bf16[1,512,256]{2,1,0:T(8,128)(2,1)}, u32[]{:S(2)}) copy-start(bf16[1,512,256]{2,1,0:T(8,128)(2,1)} %param.12) | copy-start | bytes 786436
  7.2 31.8 %copy-start.10 = (s32[8]{0:T(128)S(1)}, s32[8]{0:T(128)}, u32[]{:S(2)}) copy-start(s32[8]{0:T(128)} %param.13) | copy-start | bytes 100
  7.2 33.1 %copy-start.4 = (bf16[4096,256]{1,0:T(8,128)(2,1)S(1)}, bf16[4096,256]{1,0:T(8,128)(2,1)}, u32[]{:S(2)}) copy-start(bf16[4096,256]{1,0:T(8,128)(2,1)} %param.9) | copy-start | bytes 6291460
  7.2 145.3 %all-gather.2.cloned.1.call-start = ((), (), s32[]{:S(2)}) async-start(), calls=%async_computation.2 | async-start | bytes 17825792 | tf_op jit(solution)/shard_map/all_gather | solution.py:78
  10.5 27.4 %collective-permute-start = (bf16[128,4096]{1,0:T(8,128)(2,1)S(1)}, bf16[128,4096]{1,0:T(8,128)(2,1)S(1)}, u32[]{:S(2)}, u32[]{:S(2)}) collective-permute-start(bf16[128,4096]{1,0:T(8,128)(2,1)S(1)} %fusion.9), channel_id=1, source_target_pairs={{0,64},{64,0},{1,65},{65,1},{2,66},{66,2},{3,67},{67,3},{4,68},{68... | collective-permute-start | bytes 3145736 | tf_op jit(solution)/shard_map/ppermute | solution.py:16
  37.9 1.0 copy-start.6
  38.9 260.0 %reduce-scatter.3.cloned.1.call-start = ((), (), s32[]{:S(2)}) async-start(), calls=%async_computation.3 | async-start | bytes 17825792 | tf_op jit(solution)/shard_map/reduce_scatter | solution.py:97
  39.0 2.8 copy-start.5
  43.3 122.8 %copy-start.7 = (bf16[1,512,256]{2,1,0:T(8,128)(2,1)S(1)}, bf16[1,512,256]{2,1,0:T(8,128)(2,1)}, u32[]{:S(2)}) copy-start(bf16[1,512,256]{2,1,0:T(8,128)(2,1)} %param.11) | copy-start | bytes 786436
  166.1 4.6 %copy-start.11 = (bf16[2048,512]{1,0:T(8,128)(2,1)}, bf16[2048,512]{1,0:T(8,128)(2,1)S(1)}, u32[]{:S(2)}) copy-start(bf16[2048,512]{1,0:T(8,128)(2,1)S(1)} %convolution_convert_fusion.2) | copy-start | bytes 6291460
  167.8 4.2 %copy-start.3 = (f32[2048,512]{1,0:T(8,128)}, f32[2048,512]{1,0:T(8,128)S(1)}, u32[]{:S(2)}) copy-start(f32[2048,512]{1,0:T(8,128)S(1)} %get-tuple-element.13) | copy-start | bytes 12582916
  170.6 3.6 copy-start.12
  172.0 1.5 copy-start.8
  188.9 160.0 %reduce-scatter.5.cloned.1.call-start = ((), (), s32[]{:S(2)}) async-start(), calls=%async_computation.4 | async-start | bytes 4718592 | tf_op jit(solution)/shard_map/reduce_scatter | solution.py:109
  298.9 52.1 %collective-permute-start.1 = (bf16[128,4096]{1,0:T(8,128)(2,1)}, bf16[128,4096]{1,0:T(8,128)(2,1)}, u32[]{:S(2)}, u32[]{:S(2)}) collective-permute-start(bf16[128,4096]{1,0:T(8,128)(2,1)} %reduce-scatter.3.cloned.1.call-done), channel_id=1, source_target_pairs={{0,64},{64,0},{1,65},{65,1},{2,66},{66,2},{3,67},{67,3},{4,68},{68... | collective-permute-start | bytes 3145736 | tf_op jit(solution)/shard_map/ppermute | solution.py:16
  305.6 45.3 %copy-start.2 = (bf16[1,128,4096]{2,1,0:T(8,128)(2,1)S(1)}, bf16[1,128,4096]{2,1,0:T(8,128)(2,1)}, u32[]{:S(2)}) copy-start(bf16[1,128,4096]{2,1,0:T(8,128)(2,1)} %param.7) | copy-start | bytes 3145732
  305.7 45.3 %copy-start.9 = (f32[4096]{0:T(1024)S(1)}, f32[4096]{0:T(1024)}, u32[]{:S(2)}) copy-start(f32[4096]{0:T(1024)} %param.8) | copy-start | bytes 49156
  306.5 49.0 %copy-start.1 = (bf16[1,512,256]{2,1,0:T(8,128)(2,1)S(1)}, bf16[1,512,256]{2,1,0:T(8,128)(2,1)}, u32[]{:S(2)}) copy-start(bf16[1,512,256]{2,1,0:T(8,128)(2,1)} %param.12) | copy-start | bytes 786436
Sparse Core Ops, SparseCore 0:
  39.0 113.4 all-gather.1
  189.0 109.8 reduce-scatter.2
  301.3 47.5 reduce-scatter.4
where the time goes:
time: 363 us; the launch traced here: 362 us
  waiting for transfers between devices  266 us (73%)
  matrix products  54.7 us (15%)
  between operations  14 us (4%)
  other arithmetic  11 us (3%)
  local copies, waits for them, and re-layouts  9.37 us (3%)
  starting transfers between devices  7.45 us (2%)
    all_gather x1, waiting for transfers between devices, on_device(): gathered = lax.all_gather(partner_rows, 'seq', axis=0, tiled=True)  109 us
    reduce_scatter x1, waiting for transfers between devices, on_device(): lax.psum_scatter(lax.dot_general(kv_grads, projection, (((1,), (1,)), (()...  95.6 us
    reduce_scatter x1, waiting for transfers between devices, on_device(): lax.psum_scatter(weight_term.astype(jnp.bfloat16), ('section', 'dp'), sca...  37.9 us
    ppermute x2, waiting for transfers between devices, partner_2(): return lax.ppermute(value, axis, pairs)  22.9 us
    dot_general x1, matrix products, on_device(): lax.dot_general(kv_grads, projection, (((1,), (1,)), ((), ())), preferred...  14.6 us
    dot_general x1, matrix products, on_device(): lax.dot_general(gathered, kv_grads, (((0,), (0,)), ((), ())), preferred_e...  14.3 us
    dot_general x1, matrix products, on_device(): jnp.dot(gathered, projection, preferred_element_type=jnp.float32)  13.6 us
    ppermute x2, starting transfers between devices, partner_2(): return lax.ppermute(value, axis, pairs)  7.33 us
  transfers between devices with their start and end apart: 5, of which 4 were waited for; matrix products, arithmetic and copies ran while one was open for 8% of the time, Pallas kernels for 0%

commit v1 on v0

v1 whole, which is shorter than its diff:
```python
import functools

import jax
import jax.numpy as jnp
from jax import lax
from jax.experimental import pallas as pl
from jax.experimental.pallas import tpu as pltpu
from jax.sharding import PartitionSpec as P

D = 4096
HD = 256
TGT = 512
ROWS = 128
HALF = 64
QUART = 32
EPS = 1e-06
NEG_FILL = -1e30
MESH = pl.DeviceIdType.MESH
F32 = jnp.float32
BF16 = jnp.bfloat16
VMEM_BYTES = 60 * 1024 * 1024


class Place:
    def __init__(self):
        section, dp, seq = (lax.axis_index(a) for a in ("section", "dp", "seq"))
        self.x, self.y = seq // 4, seq % 4
        self.core = dp % 2
        self.z = section * 2 + dp // 2
        self.position = section * 4 + dp
        x, y, z, core = self.x, self.y, self.z, self.core
        self.ky = y // 2
        self.group = (y % 2 + y // 2) % 2
        self.xp = (section, dp, ((x + 1) % 4) * 4 + y)
        self.xm = (section, dp, ((x + 3) % 4) * 4 + y)
        self.yn = (section, dp, x * 4 + 3 - y)
        self.pair = (section, dp, x * 4 + y + 1 - 2 * (y % 2))
        self.sib = (section, dp + 1 - 2 * core, seq)
        zp, zm = (z + 1) % 4, (z + 3) % 4
        self.zp = (zp // 2, (zp % 2) * 2 + core, seq)
        self.zm = (zm // 2, (zm % 2) * 2 + core, seq)
        self.across = (1 - section, dp, seq)

    def slot(self, dx, w):
        return ((self.x + dx) % 4) * 2 + (self.ky if w == 0 else 1 - self.ky)

    def enter(self):
        everyone = (
            self.xp,
            self.xm,
            self.yn,
            self.pair,
            self.sib,
            self.zp,
            self.zm,
            self.across,
        )
        barrier = pltpu.get_barrier_semaphore()
        for device in everyone:
            pl.semaphore_signal(barrier, inc=1, device_id=device, device_id_type=MESH)
        pl.semaphore_wait(barrier, len(everyone))


def remote(src, dst, send, recv, device):
    return pltpu.make_async_remote_copy(
        src_ref=src,
        dst_ref=dst,
        send_sem=send,
        recv_sem=recv,
        device_id=device,
        device_id_type=MESH,
    )


def at(start, size, unit):
    return pl.ds(pl.multiple_of(start, unit), size)


class Wires:
    def __init__(self, send, recv, home):
        self.send, self.recv, self.home = send, recv, home
        self.open = []

    def put(self, i, src, dst, device):
        copy = remote(src, dst, self.send.at[i], self.recv.at[i], device)
        copy.start()
        self.open.append(copy)

    def got(self, i, dst):
        remote(dst, dst, self.send.at[i], self.recv.at[i], self.home).wait_recv()

    def close(self):
        for copy in self.open:
            copy.wait_send()


GATHER_GOT = (
    (-1, 0, 0, 64),
    (1, 0, 0, 64),
    (2, 0, 0, 32),
    (2, 0, 32, 32),
    (0, 1, 0, 64),
    (-1, 1, 0, 64),
    (1, 1, 0, 64),
    (2, 1, 0, 64),
    (0, 1, 64, 64),
    (-1, 0, 64, 64),
    (1, 0, 64, 64),
    (2, 0, 64, 32),
    (2, 0, 96, 32),
    (-1, 1, 64, 64),
    (1, 1, 64, 64),
    (2, 1, 64, 32),
    (2, 1, 96, 32),
)
GATHER_PUT = (
    (0, 0, 0, 64, "xp"),
    (0, 0, 0, 64, "xm"),
    (-1, 0, 0, 32, "xp"),
    (1, 0, 32, 32, "xm"),
    (0, 0, 0, 64, "yn"),
    (-1, 0, 0, 64, "yn"),
    (1, 0, 0, 64, "yn"),
    (2, 0, 0, 64, "yn"),
    (0, 0, 64, 64, "yn"),
    (0, 0, 64, 64, "xp"),
    (0, 0, 64, 64, "xm"),
    (-1, 0, 64, 32, "xp"),
    (1, 0, 96, 32, "xm"),
    (0, 1, 64, 64, "xp"),
    (0, 1, 64, 64, "xm"),
    (-1, 1, 64, 32, "xp"),
    (1, 1, 96, 32, "xm"),
)


def forward_kernel(
    len_ref, enc, gain, kw, vw, q, g,
    xg_out, wp_out, att, dq, kvg,
    xg, w, wp, kv, kvs, qr, gr, pbuf, sbuf,
    xs, xr, ws, wr, cs, cr, loc,
):
    me = Place()
    load_k = pltpu.make_async_copy(kw, w.at[:, 0:HD], loc.at[0])
    load_v = pltpu.make_async_copy(vw, w.at[:, HD : 2 * HD], loc.at[1])
    load_k.start()
    load_v.start()
    me.enter()

    rows = Wires(xs, xr, me.xp)
    weights = Wires(ws, wr, me.zp)
    heads = Wires(cs, cr, me.pair)

    def piece(spec):
        return xg.at[at(me.slot(spec[0], spec[1]) * ROWS + spec[2], spec[3], 32)]

    def put(*ids):
        for i in ids:
            spec = GATHER_PUT[i]
            rows.put(i, piece(spec), piece(spec), getattr(me, spec[4]))

    def got(*ids):
        for i in ids:
            rows.got(i, piece(GATHER_GOT[i]))

    def slice_of(dz, sibling, first=0, count=512):
        z = (me.z + dz) % 4
        c = 1 - me.core if sibling else me.core
        return wp.at[at((z * 2 + c) * 512 + first, count, 256)]

    mine = me.position * 512
    weights.put(0, kw.at[at(mine, 512, 512)], wp.at[at(mine, 512, 512), 0:HD], me.pair)
    weights.put(1, vw.at[at(mine, 512, 512)], wp.at[at(mine, 512, 512), HD : 2 * HD], me.pair)

    own = me.slot(0, 0) * ROWS

    def norm_rows(i, _):
        wide = enc[at(i * 32, 32, 32), :].astype(F32)
        factor = lax.rsqrt(jnp.mean(wide * wide, axis=-1, keepdims=True) + EPS)
        xg[at(own + i * 32, 32, 32), :] = (wide * factor * gain[...]).astype(BF16)
        return 0

    lax.fori_loop(0, ROWS // 32, norm_rows, 0)
    put(0, 1, 8, 9, 10, 4)

    def project(row, count, matrix, out):
        block = at(row, count, 128)
        out[block, :] = jnp.dot(
            xg[block, :], matrix[...], preferred_element_type=F32
        ).astype(BF16)

    def column(dx):
        return ((me.x + dx) % 4) * 2 * ROWS

    def give_heads(i, row, count):
        block = at(row, count, 128)
        heads.put(i, kvs.at[block], kv.at[at(row + 1024, count, 128)], me.pair)

    weights.got(0, wp.at[at(mine, 512, 512), 0:HD])
    weights.got(1, wp.at[at(mine, 512, 512), HD : 2 * HD])
    weights.put(2, slice_of(0, 0), slice_of(0, 0), me.zp)
    weights.put(3, slice_of(0, 0), slice_of(0, 0), me.zm)
    weights.put(6, slice_of(0, 0), slice_of(0, 0), me.sib)

    got(0)
    put(2, 5)
    got(1)
    put(3, 6)
    got(8)
    put(13, 14)
    weights.got(2, slice_of(-1, 0))
    weights.put(4, slice_of(-1, 0, 0, 256), slice_of(-1, 0, 0, 256), me.zp)
    weights.put(7, slice_of(-1, 0), slice_of(-1, 0), me.sib)
    weights.got(3, slice_of(1, 0))
    weights.put(5, slice_of(1, 0, 256, 256), slice_of(1, 0, 256, 256), me.zm)
    weights.put(8, slice_of(1, 0), slice_of(1, 0), me.sib)
    weights.put(10, q, qr, me.across)
    weights.put(11, g, gr, me.across)
    got(9)
    put(11)
    got(10)
    put(12)
    got(2, 3)
    put(7)
    got(4)
    load_k.wait()
    load_v.wait()
    project(column(0), 256, w, kv)
    weights.got(4, slice_of(2, 0, 0, 256))
    weights.got(5, slice_of(2, 0, 256, 256))
    weights.put(9, slice_of(2, 0), slice_of(2, 0), me.sib)
    for i, dz in enumerate((0, -1, 1, 2)):
        weights.got(6 + i, slice_of(dz, 1))
    keep_w = pltpu.make_async_copy(wp, wp_out, loc.at[2])
    keep_w.start()
    project(column(0), 256, wp, kvs)
    give_heads(0, column(0), 256)
    got(13)
    put(15)
    got(14)
    put(16)
    got(5)
    project(column(-1), 256, wp, kvs)
    give_heads(1, column(-1), 256)
    project(column(-1), 256, w, kv)
    got(6)
    project(column(1), 256, wp, kvs)
    give_heads(2, column(1), 256)
    project(column(1), 256, w, kv)
    got(11, 12)
    far = me.slot(2, 0) * ROWS
    project(far, 128, wp, kvs)
    give_heads(3, far, 128)
    project(far, 128, w, kv)
    got(15, 16, 7)
    last = me.slot(2, 1) * ROWS
    project(last, 128, wp, kvs)
    give_heads(4, last, 128)
    keep_x = pltpu.make_async_copy(xg, xg_out, loc.at[3])
    keep_x.start()
    project(last, 128, w, kv)
    weights.got(10, qr)
    weights.got(11, gr)

    for i, (start, count) in enumerate(
        ((column(0), 256), (column(-1), 256), (column(1), 256), (far, 128), (last, 128))
    ):
        heads.got(i, kv.at[at(start + 1024, count, 128)])

    length = len_ref[me.position]
    lane = lax.broadcasted_iota(jnp.int32, (1, 2048), 1)
    block = (lane % 1024) // ROWS
    group = (me.group + lane // 1024) % 2
    row_y = group + (block % 2) * (3 - 2 * group)
    visible = ((block // 2) * 4 + row_y) * ROWS + lane % ROWS < length
    scale = HD**-0.5
    nt = (((1,), (1,)), ((), ()))
    tn = (((0,), (0,)), ((), ()))

    def attend(i, _):
        part = at(i * 128, 128, 128)
        scores = lax.dot_general(qr[part, :], kv[:, 0:HD], nt, preferred_element_type=F32)
        scores = jnp.where(visible, scores * scale, NEG_FILL)
        top = jnp.max(scores, axis=-1, keepdims=True)
        exponent = jnp.exp(scores - top)
        total = jnp.sum(exponent, axis=-1, keepdims=True)
        probs = exponent * (1.0 / total)
        weights16 = probs.astype(BF16)
        pbuf[part, :] = weights16
        att[part, :] = jnp.dot(
            weights16, kv[:, HD : 2 * HD], preferred_element_type=F32
        ).astype(BF16)
        grad_probs = lax.dot_general(
            gr[part, :], kv[:, HD : 2 * HD], nt, preferred_element_type=F32
        )
        inner = jnp.sum(probs * grad_probs, axis=-1, keepdims=True)
        grad_scores = (probs * (grad_probs - inner) * scale).astype(BF16)
        sbuf[part, :] = grad_scores
        dq[part, :] = jnp.dot(
            grad_scores, kv[:, 0:HD], preferred_element_type=F32
        ).astype(BF16)
        return 0

    lax.fori_loop(0, TGT // 128, attend, 0)

    def transposed(i, _):
        part = at(i * 512, 512, 512)
        kvg[part, 0:HD] = lax.dot_general(
            sbuf[:, part], qr[...], tn, preferred_element_type=F32
        ).astype(BF16)
        kvg[part, HD : 2 * HD] = lax.dot_general(
            pbuf[:, part], gr[...], tn, preferred_element_type=F32
        ).astype(BF16)
        return 0

    lax.fori_loop(0, 4, transposed, 0)

    rows.close()
    weights.close()
    heads.close()
    keep_w.wait()
    keep_x.wait()


Y_TOP = {2: 0, 1: 64, -1: 128, 0: 192}
RINGS = {"top": 256, "low0": 448, "low1": 640}
Y_LOW = 832


def backward_kernel(
    enc, gain, kw, vw, wp_in, xg, kvg, att_in, dq_in,
    enc_grad, kg, vg, att, dq,
    w, wp, x, r, rbuf, kvp, kt, gs, gb, zb, pb, ps, kvv,
    rs, rr, gss, gsr, zs, zr, hs, hr, loc,
):
    me = Place()
    loads = [
        pltpu.make_async_copy(kw, w.at[:, 0:HD], loc.at[0]),
        pltpu.make_async_copy(vw, w.at[:, HD : 2 * HD], loc.at[1]),
        pltpu.make_async_copy(wp_in, wp, loc.at[2]),
        pltpu.make_async_copy(xg, x, loc.at[3]),
    ]
    load_kv = pltpu.make_async_copy(kvg, kvv, loc.at[4])
    load_kv.start()
    for load in loads:
        load.start()
    me.enter()

    rows = Wires(rs, rr, me.xp)
    near = Wires(gss, gsr, me.sib)
    rings = Wires(zs, zr, me.zp)
    heads = Wires(hs, hr, me.pair)
    nt = (((1,), (1,)), ((), ()))

    def column(dx):
        return ((me.x + dx) % 4) * 2 * ROWS

    load_kv.wait()
    order = (2, 1, -1, 0)
    for i, dx in enumerate(order):
        heads.put(
            i,
            kvv.at[at(column(dx) + 1024, 256, 256)],
            kvp.at[at(column(dx), 256, 256)],
            me.pair,
        )
    heads.put(5, att_in, att, me.across)
    heads.put(6, dq_in, dq, me.across)
    kt[0] = kvv[0:1024, :].T
    for load in loads[:3]:
        load.wait()

    def row_terms(dx):
        block = at(column(dx), 256, 256)
        heads.got(order.index(dx), kvp.at[block])

        def tile(n, _):
            cols = at(n * 512, 512, 512)
            total = lax.dot_general(kvv[block, :], w[cols, :], nt, preferred_element_type=F32)
            total += lax.dot_general(kvp[block, :], wp[cols, :], nt, preferred_element_type=F32)
            r[block, cols] = total.astype(BF16)
            return 0

        lax.fori_loop(0, D // 512, tile, 0)

    def rows_of(dx, w_, first, count):
        return at(me.slot(dx, w_) * ROWS + first, count, 32)

    def add(target, source, count):
        def part(i, _):
            to, of = at(target + i * 16, 16, 16), at(source + i * 16, 16, 16)
            r[to, :] = (r[to, :].astype(F32) + rbuf[of, :].astype(F32)).astype(BF16)
            return 0

        lax.fori_loop(0, count // 16, part, 0)

    def y_top(dx):
        i = order.index(dx)
        rows.put(
            i, r.at[rows_of(dx, 1, 0, 64)], rbuf.at[Y_TOP[dx] : Y_TOP[dx] + 64], me.yn
        )

    def y_top_add(dx):
        i = order.index(dx)
        rows.got(i, rbuf.at[Y_TOP[dx] : Y_TOP[dx] + 64])
        add(me.slot(dx, 0) * ROWS, Y_TOP[dx], 64)

    ring_of = {"top": (0, 0, 4), "low0": (0, 64, 8), "low1": (1, 64, 12)}

    def ring_first(name):
        w_, first, i = ring_of[name]
        base = RINGS[name]
        rows.put(i, r.at[rows_of(2, w_, first, 32)], rbuf.at[base : base + 32], me.xp)
        rows.put(
            i + 1, r.at[rows_of(2, w_, first + 32, 32)], rbuf.at[base + 32 : base + 64], me.xm
        )

    def ring_second(name):
        w_, first, i = ring_of[name]
        base = RINGS[name]
        rows.got(i, rbuf.at[base : base + 32])
        add(me.slot(1, w_) * ROWS + first, base, 32)
        rows.put(
            i + 2, r.at[rows_of(1, w_, first, 64)], rbuf.at[base + 64 : base + 128], me.xp
        )
        rows.got(i + 1, rbuf.at[base + 32 : base + 64])
        add(me.slot(-1, w_) * ROWS + first + 32, base + 32, 32)
        rows.put(
            i + 3, r.at[rows_of(-1, w_, first, 64)], rbuf.at[base + 128 : base + 192], me.xm
        )

    def ring_wait(name):
        _, _, i = ring_of[name]
        base = RINGS[name]
        rows.got(i + 2, rbuf.at[base + 64 : base + 128])
        rows.got(i + 3, rbuf.at[base + 128 : base + 192])

    def grad_term(h, dz, sibling):
        z = (me.z + dz) % 4
        c = 1 - me.core if sibling else me.core
        return jnp.dot(
            kt[h], x[:, at((z * 2 + c) * 512, 512, 512)], preferred_element_type=F32
        )

    def near_put(h, n, dz):
        gs[h * 4 + n] = grad_term(h, dz, 1).astype(BF16)
        near.put(h * 4 + n, gs.at[h * 4 + n], gb.at[h * 4 + n], me.sib)

    def near_add(h, n, dz):
        term = grad_term(h, dz, 0)
        near.got(h * 4 + n, gb.at[h * 4 + n])
        gb[h * 4 + n] = (gb[h * 4 + n].astype(F32) + term).astype(BF16)

    def z_first(h):
        rings.put(h * 4, gb.at[h * 4, 0:256], zb.at[h, 0:256], me.zp)
        rings.put(h * 4 + 1, gb.at[h * 4, 256:512], zb.at[h, 256:512], me.zm)

    def z_second(h):
        rings.got(h * 4, zb.at[h, 0:256])
        gb[h * 4 + 1, 0:256] = (
            gb[h * 4 + 1, 0:256].astype(F32) + zb[h, 0:256].astype(F32)
        ).astype(BF16)
        rings.put(h * 4 + 2, gb.at[h * 4 + 1], zb.at[h, 512:1024], me.zp)
        rings.got(h * 4 + 1, zb.at[h, 256:512])
        gb[h * 4 + 2, 256:512] = (
            gb[h * 4 + 2, 256:512].astype(F32) + zb[h, 256:512].astype(F32)
        ).astype(BF16)
        rings.put(h * 4 + 3, gb.at[h * 4 + 2], zb.at[h, 1024:1536], me.zm)

    def z_sum(h):
        rings.got(h * 4 + 2, zb.at[h, 512:1024])
        rings.got(h * 4 + 3, zb.at[h, 1024:1536])
        return (
            gb[h * 4 + 3].astype(F32)
            + zb[h, 512:1024].astype(F32)
            + zb[h, 1024:1536].astype(F32)
        )

    row_terms(2)
    y_top(2)
    ring_first("low1")
    ring_first("low0")
    loads[3].wait()
    near_put(0, 0, 2)
    near_add(0, 0, 2)
    z_first(0)
    row_terms(1)
    y_top(1)
    near_put(0, 1, 1)
    near_put(0, 2, -1)
    row_terms(-1)
    y_top(-1)
    ring_second("low1")
    y_top_add(2)
    ring_first("top")
    near_add(0, 1, 1)
    near_add(0, 2, -1)
    z_second(0)
    row_terms(0)
    y_top(0)
    ring_second("low0")
    near_put(0, 3, 0)
    kt[1] = kvp[...].T
    near_put(1, 0, 2)
    near_put(1, 1, 1)
    near_put(1, 2, -1)
    near_put(1, 3, 0)
    near_add(1, 0, 2)
    z_first(1)
    near_add(0, 3, 0)
    near_add(1, 1, 1)
    near_add(1, 2, -1)
    near_add(1, 3, 0)
    y_top_add(1)
    y_top_add(-1)
    ring_second("top")
    ring_wait("low1")
    base = RINGS["low1"]
    add(me.slot(0, 1) * ROWS + 64, base + 64, 64)
    add(me.slot(0, 1) * ROWS + 64, base + 128, 64)
    rows.put(16, r.at[rows_of(0, 1, 64, 64)], rbuf.at[Y_LOW : Y_LOW + 64], me.yn)
    z_second(1)
    ps[...] = z_sum(1).astype(BF16)
    heads.put(4, ps, pb, me.pair)
    own_sum = z_sum(0)
    heads.got(4, pb)
    total = own_sum + pb[...].astype(F32)
    kg[...] = total[0:HD, :].T
    vg[...] = total[HD : 2 * HD, :].T

    own = me.slot(0, 0) * ROWS
    rows.got(3, rbuf.at[Y_TOP[0] : Y_TOP[0] + 64])
    ring_wait("low0")
    ring_wait("top")
    rows.got(16, rbuf.at[Y_LOW : Y_LOW + 64])

    def finish(first, ring, extra):
        def part(i, _):
            here = at(own + first + i * 16, 16, 16)
            grad = r[here, :].astype(F32)
            for start in (ring + 64, ring + 128, extra):
                grad += rbuf[at(start + i * 16, 16, 16), :].astype(F32)
            out = at(first + i * 16, 16, 16)
            wide = enc[out, :].astype(F32)
            factor = lax.rsqrt(jnp.mean(wide * wide, axis=-1, keepdims=True) + EPS)
            scaled = grad.astype(BF16).astype(F32) * gain[...]
            inner = jnp.mean(scaled * wide, axis=-1, keepdims=True)
            enc_grad[out, :] = (
                factor * scaled - wide * (factor * factor * factor * inner)
            ).astype(BF16)
            return 0

        lax.fori_loop(0, 4, part, 0)

    finish(0, RINGS["top"], Y_TOP[0])
    finish(64, RINGS["low0"], Y_LOW)

    heads.got(5, att)
    heads.got(6, dq)
    rows.close()
    near.close()
    rings.close()
    heads.close()


def on_device(enc_states, enc_gain, key_weight, value_weight, queries, out_grad, lengths):
    enc = enc_states[0]
    gain = enc_gain.reshape(1, D)
    vmem = pl.BlockSpec(memory_space=pltpu.VMEM)
    far = pl.BlockSpec(memory_space=pl.ANY)
    dma = pltpu.SemaphoreType.DMA
    shape = jax.ShapeDtypeStruct

    def params(i):
        return pltpu.CompilerParams(
            collective_id=i, has_side_effects=True, vmem_limit_bytes=VMEM_BYTES
        )

    xg, wp, att, dq, kvg = pl.pallas_call(
        forward_kernel,
        out_shape=(
            shape((1024, D), BF16),
            shape((D, 2 * HD), BF16),
            shape((TGT, HD), BF16),
            shape((TGT, HD), BF16),
            shape((2048, 2 * HD), BF16),
        ),
        in_specs=[pl.BlockSpec(memory_space=pltpu.SMEM), vmem, vmem, far, far, far, far],
        out_specs=(far, far, vmem, vmem, vmem),
        scratch_shapes=[
            pltpu.VMEM((1024, D), BF16),
            pltpu.VMEM((D, 2 * HD), BF16),
            pltpu.VMEM((D, 2 * HD), BF16),
            pltpu.VMEM((2048, 2 * HD), BF16),
            pltpu.VMEM((1024, 2 * HD), BF16),
            pltpu.VMEM((TGT, HD), BF16),
            pltpu.VMEM((TGT, HD), BF16),
            pltpu.VMEM((TGT, 2048), BF16),
            pltpu.VMEM((TGT, 2048), BF16),
            dma((17,)),
            dma((17,)),
            dma((12,)),
            dma((12,)),
            dma((5,)),
            dma((5,)),
            dma((4,)),
        ],
        compiler_params=params(0),
        name="gather_project_attend",
    )(lengths, enc, gain, key_weight, value_weight, queries[0], out_grad[0])

    enc_grad, kg, vg, att, dq = pl.pallas_call(
        backward_kernel,
        out_shape=(
            shape((ROWS, D), BF16),
            shape((512, HD), F32),
            shape((512, HD), F32),
            shape((TGT, HD), BF16),
            shape((TGT, HD), BF16),
        ),
        in_specs=[vmem, vmem] + [far] * 7,
        out_specs=(vmem, vmem, vmem, far, far),
        scratch_shapes=[
            pltpu.VMEM((D, 2 * HD), BF16),
            pltpu.VMEM((D, 2 * HD), BF16),
            pltpu.VMEM((1024, D), BF16),
            pltpu.VMEM((1024, D), BF16),
            pltpu.VMEM((896, D), BF16),
            pltpu.VMEM((1024, 2 * HD), BF16),
            pltpu.VMEM((2, 2 * HD, 1024), BF16),
            pltpu.VMEM((8, 512, 512), BF16),
            pltpu.VMEM((8, 512, 512), BF16),
            pltpu.VMEM((2, 1536, 512), BF16),
            pltpu.VMEM((512, 512), BF16),
            pltpu.VMEM((512, 512), BF16),
            pltpu.VMEM((2048, 2 * HD), BF16),
            dma((17,)),
            dma((17,)),
            dma((8,)),
            dma((8,)),
            dma((8,)),
            dma((8,)),
            dma((7,)),
            dma((7,)),
            dma((5,)),
        ],
        compiler_params=params(1),
        name="row_and_weight_grads",
    )(enc, gain, key_weight, value_weight, wp, xg, kvg, att, dq)
    return (att[None], enc_grad[None], kg, vg, dq[None])


def solution(mesh):
    placed = (
        P(("section", "dp"), "seq", None),
        P(),
        P(None, "seq"),
        P(None, "seq"),
        P(("section", "dp"), None, "seq"),
        P(("section", "dp"), None, "seq"),
        P(),
    )
    return jax.shard_map(
        on_device,
        mesh=mesh,
        in_specs=placed,
        out_specs=(
            P(("section", "dp"), None, "seq"),
            P(("section", "dp"), "seq", None),
            P(("section", "dp"), "seq"),
            P(("section", "dp"), "seq"),
            P(("section", "dp"), None, "seq"),
        ),
        check_vma=False,
    )
```

time: 363 us -> 179 us (0.49)
  waiting for transfers between devices: 266 us -> 0 us
  Pallas kernels: 0 us -> 171 us
  matrix products: 54.7 us -> 0 us
  between operations: 14 us -> 0.67 us
  other arithmetic: 11 us -> 0 us
  starting transfers between devices: 7.45 us -> 0 us
    pallas_call x0 -> x2, Pallas kernels: none -> 171 us  [the longest x1 88.2 us: on_device(): pl.pallas_call(forward_kernel, out_shape=(shape((1024, D), BF16), shape((...]
    reduce_scatter x2 -> x0, waiting for transfers between devices: 133 us -> none  [the longest x1 95.6 us: on_device(): lax.psum_scatter(lax.dot_general(kv_grads, projection, (((1,), (1,)), (()...]
    all_gather x1 -> x0, waiting for transfers between devices: 109 us -> none  [on_device(): gathered = lax.all_gather(partner_rows, 'seq', axis=0, tiled=True)]
    dot_general x9 -> x0, matrix products: 54.7 us -> none  [the longest x1 14.6 us: on_device(): lax.dot_general(kv_grads, projection, (((1,), (1,)), ((), ())), preferred...]
    ppermute x2 -> x0, waiting for transfers between devices: 22.9 us -> none  [partner_2(): return lax.ppermute(value, axis, pairs)]
    ppermute x2 -> x0, starting transfers between devices: 7.33 us -> none  [partner_2(): return lax.ppermute(value, axis, pairs)]
    reduce_sum x3 -> x0, other arithmetic: 4.34 us -> none  [the longest x1 1.67 us: normalize(): jnp.mean(wide_rows * wide_rows, axis=-1, keepdims=True) + EPS]
  transfers between devices with their start and end apart: 5 -> 0, of which waited for: 4 -> 0; matrix products, arithmetic and copies ran while one was open for 8% -> 0% of each run, Pallas kernels for 0% -> 0%
where the time goes in v1:
time: 179 us; the launch traced here: 178 us
  Pallas kernels  171 us (96%)
  local copies, waits for them, and re-layouts  6.39 us (4%)
    pallas_call x1, Pallas kernels, on_device(): pl.pallas_call(forward_kernel, out_shape=(shape((1024, D), BF16), shape((...  88.2 us
    pallas_call x1, Pallas kernels, on_device(): pl.pallas_call(backward_kernel, out_shape=(shape((ROWS, D), BF16), shape(...  83.2 us
    unnamed x11, local copies, waits for them, and re-layouts  6.39 us

profile of v1, /device:TPU:1, one launch (start us, length us, event | category | flops | bytes accessed | tf_op | source)
XLA Modules:
  0.0 178.5 jit_solution(16131507565727125864)
XLA Ops:
  0.6 88.2 %gather_project_attend.1 = (bf16[1024,4096]{1,0:T(8,128)(2,1)}, bf16[4096,512]{1,0:T(8,128)(2,1)}, bf16[512,256]{1,0:T(8,128)(2,1)}, bf16[512,256]{1,0:T(8,128)(2,1)}, bf16[2048,512]{1,0:T(8,128)(2,1)}) custom-call(s32[8]{0:T(128)} %len_ref.1, bf16[128,4096]{1,0:T(8,128)(2,1)} %bitcast.7, f32[1,4096]{1,0:T(1,128)} %bitcast.14, bf16[4096,256]{1,0:T(8,128)(2,1)} %kw.3, ...), custom_call_target="tpu_custom_call" | custom-call | tf_op jit(solution)/shard_map/gather_project_attend/pallas_call | solution.py:579
  88.9 83.2 %row_and_weight_grads.1 = (bf16[128,4096]{1,0:T(8,128)(2,1)}, f32[512,256]{1,0:T(8,128)}, f32[512,256]{1,0:T(8,128)}, bf16[512,256]{1,0:T(8,128)(2,1)}, bf16[512,256]{1,0:T(8,128)(2,1)}) custom-call(bf16[128,4096]{1,0:T(8,128)(2,1)} %bitcast.8, f32[1,4096]{1,0:T(1,128)} %bitcast.15, bf16[4096,256]{1,0:T(8,128)(2,1)} %kw.3, bf16[4096,256]{1,0:T(8,128)(2,1)} %vw.3, ...), custom_call_target="tpu_custom_call" | custom-call | tf_op jit(solution)/shard_map/row_and_weight_grads/pallas_call | solution.py:612
  172.1 0.0 copy-start.1
  172.1 0.0 copy-start
  172.1 1.8 copy.17
  173.8 0.0 copy-start.2
  173.8 2.3 %copy.18 = bf16[1,128,4096]{2,1,0:T(8,128)(2,1)} copy(bf16[1,128,4096]{2,1,0:T(8,128)(2,1)} %bitcast.9) | data formatting | bytes 2097152
  176.2 0.0 copy-done.1
  176.2 0.8 copy.19
  177.0 0.0 copy-done
  177.0 0.8 copy.20
  177.8 0.0 copy-done.2
  177.8 0.7 copy.21
Async XLA Ops:
  172.1 4.1 %copy-start.1 = (f32[512,256]{1,0:T(8,128)S(1)}, f32[512,256]{1,0:T(8,128)}, u32[]{:S(2)}) copy-start(f32[512,256]{1,0:T(8,128)} %get-tuple-element.32) | copy-start | bytes 1572868
  172.1 4.9 %copy-start = (f32[512,256]{1,0:T(8,128)S(1)}, f32[512,256]{1,0:T(8,128)}, u32[]{:S(2)}) copy-start(f32[512,256]{1,0:T(8,128)} %get-tuple-element.33) | copy-start | bytes 1572868
  173.8 3.9 %copy-start.2 = (bf16[512,256]{1,0:T(8,128)(2,1)S(1)}, bf16[512,256]{1,0:T(8,128)(2,1)}, u32[]{:S(2)}) copy-start(bf16[512,256]{1,0:T(8,128)(2,1)} %get-tuple-element.24) | copy-start | bytes 786436

commit v2 on v0

v2 whole, which is shorter than its diff:
```python
import jax
import jax.numpy as jnp
from jax import lax
from jax.experimental import pallas as pl
from jax.experimental.pallas import tpu as pltpu
from jax.sharding import PartitionSpec as P

D = 4096
HD = 256
TGT = 512
ROWS = 128
EPS = 1e-06
NEG_FILL = -1e30
MESH = pl.DeviceIdType.MESH
F32 = jnp.float32
BF16 = jnp.bfloat16
VMEM_BYTES = 62 * 1024 * 1024
NT = (((1,), (1,)), ((), ()))
TN = (((0,), (0,)), ((), ()))
CUT = 1792
TOP = (0, CUT)
TOP_A, TOP_B = (0, CUT // 2), (CUT // 2, CUT // 2)
LOW = (CUT, D - CUT)
LOW_A, LOW_B = (CUT, (D - CUT) // 2), (CUT + (D - CUT) // 2, (D - CUT) // 2)


class Place:
    def __init__(self):
        section, dp, seq = (lax.axis_index(a) for a in ("section", "dp", "seq"))
        self.x, self.y = seq // 4, seq % 4
        self.core = dp % 2
        self.z = section * 2 + dp // 2
        self.position = section * 4 + dp
        x, y, z, core = self.x, self.y, self.z, self.core
        self.ky = y // 2
        self.group = (y % 2 + y // 2) % 2
        self.xp = (section, dp, ((x + 1) % 4) * 4 + y)
        self.xm = (section, dp, ((x + 3) % 4) * 4 + y)
        self.yn = (section, dp, x * 4 + 3 - y)
        self.pair = (section, dp, x * 4 + y + 1 - 2 * (y % 2))
        self.sib = (section, dp + 1 - 2 * core, seq)
        zp, zm = (z + 1) % 4, (z + 3) % 4
        self.zp = (zp // 2, (zp % 2) * 2 + core, seq)
        self.zm = (zm // 2, (zm % 2) * 2 + core, seq)
        self.across = (1 - section, dp, seq)

    def column(self, dx):
        return ((self.x + dx) % 4) * 2 * ROWS

    def block(self, dx, w):
        return self.column(dx) + (self.ky if w == 0 else 1 - self.ky) * ROWS

    def enter(self):
        everyone = (
            self.xp,
            self.xm,
            self.yn,
            self.pair,
            self.sib,
            self.zp,
            self.zm,
            self.across,
        )
        barrier = pltpu.get_barrier_semaphore()
        for device in everyone:
            pl.semaphore_signal(barrier, inc=1, device_id=device, device_id_type=MESH)
        pl.semaphore_wait(barrier, len(everyone))


def at(start, size, unit=None):
    return pl.ds(pl.multiple_of(start, unit or min(size, 256)), size)


class Wires:
    def __init__(self, send, recv, home):
        self.send, self.recv, self.home = send, recv, home
        self.open = {}

    def copy(self, i, src, dst, device):
        return pltpu.make_async_remote_copy(
            src_ref=src,
            dst_ref=dst,
            send_sem=self.send.at[i],
            recv_sem=self.recv.at[i],
            device_id=device,
            device_id_type=MESH,
        )

    def put(self, i, src, dst, device):
        self.copy(i, src(), dst(), device).start()
        self.open[i] = src

    def got(self, i, dst):
        self.copy(i, dst(), dst(), self.home).wait_recv()

    def close(self):
        for i, src in self.open.items():
            self.copy(i, src(), src(), self.home).wait_send()


GATHER_GOT = (
    (-1, 0, TOP),
    (1, 0, TOP),
    (2, 0, TOP_A),
    (2, 0, TOP_B),
    (0, 1, TOP),
    (-1, 1, TOP),
    (1, 1, TOP),
    (2, 1, TOP),
    (0, 1, LOW),
    (-1, 0, LOW),
    (1, 0, LOW),
    (2, 0, LOW_A),
    (2, 0, LOW_B),
    (-1, 1, LOW),
    (1, 1, LOW),
    (2, 1, LOW_A),
    (2, 1, LOW_B),
)
GATHER_PUT = (
    (0, 0, TOP, "xp"),
    (0, 0, TOP, "xm"),
    (-1, 0, TOP_A, "xp"),
    (1, 0, TOP_B, "xm"),
    (0, 0, TOP, "yn"),
    (-1, 0, TOP, "yn"),
    (1, 0, TOP, "yn"),
    (2, 0, TOP, "yn"),
    (0, 0, LOW, "yn"),
    (0, 0, LOW, "xp"),
    (0, 0, LOW, "xm"),
    (-1, 0, LOW_A, "xp"),
    (1, 0, LOW_B, "xm"),
    (0, 1, LOW, "xp"),
    (0, 1, LOW, "xm"),
    (-1, 1, LOW_A, "xp"),
    (1, 1, LOW_B, "xm"),
)
ORDER = (2, 1, -1, 0)


def kernel(
    len_ref, enc, gain, kw, vw, q, g,
    row_grad, col_grad, att_out, dq_out,
    xg, w, wp, kv, kvs, qr, gr, pbuf, sbuf, att, dq, kvg, kvp, kt,
    r, yt, ta, tc, la, lc, yl, gb, zb, ps, pb,
    xs, xr, ws, wr, hs, hr, bs, br, ns, nr, zs, zr, loc, gate,
):
    me = Place()
    load_k = pltpu.make_async_copy(kw, w.at[:, 0:HD], loc.at[0])
    load_v = pltpu.make_async_copy(vw, w.at[:, HD : 2 * HD], loc.at[1])
    load_k.start()
    load_v.start()
    me.enter()

    rows = Wires(xs, xr, me.xp)
    weights = Wires(ws, wr, me.zp)
    heads = Wires(hs, hr, me.pair)
    back = Wires(bs, br, me.xp)
    near = Wires(ns, nr, me.sib)
    rings = Wires(zs, zr, me.zp)

    def core(c):
        return pl.when(me.core == c)


    def part(ref, row, cols):
        return lambda: ref.at[at(row(), ROWS), cols[0] : cols[0] + cols[1]]

    def piece(spec):
        return part(xg, lambda: me.block(spec[0], spec[1]), spec[2])

    def put(*ids):
        for i in ids:
            spec = GATHER_PUT[i]
            rows.put(i, piece(spec), piece(spec), getattr(me, spec[3]))

    def got(*ids):
        for i in ids:
            rows.got(i, piece(GATHER_GOT[i]))

    def slice_of(dz, sibling, first=0, count=512):
        z = (me.z + dz) % 4
        c = 1 - me.core if sibling else me.core
        return lambda: wp.at[at((z * 2 + c) * 512 + first, count)]

    def whole(ref):
        return lambda: ref

    mine = me.position * 512
    key_slice = lambda: wp.at[at(mine, 512), 0:HD]
    value_slice = lambda: wp.at[at(mine, 512), HD : 2 * HD]
    weights.put(0, lambda: kw.at[at(mine, 512)], key_slice, me.pair)
    weights.put(1, lambda: vw.at[at(mine, 512)], value_slice, me.pair)
    weights.put(10, whole(q), whole(qr), me.across)
    weights.put(11, whole(g), whole(gr), me.across)

    own = me.block(0, 0)

    def norm_rows(i, _):
        wide = enc[at(i * 32, 32), :].astype(F32)
        factor = lax.rsqrt(jnp.mean(wide * wide, axis=-1, keepdims=True) + EPS)
        xg[at(own + i * 32, 32), :] = (wide * factor * gain[...]).astype(BF16)
        return 0

    lax.fori_loop(0, ROWS // 32, norm_rows, 0)

    def begin():
        put(0, 1, 8, 9, 10, 4)

    def relay_first():
        got(8)
        put(13, 14)
        got(0)
        put(2, 5)
        got(1)
        put(3, 6)

    def relay_second():
        got(9)
        put(11)
        got(10)
        put(12)
        got(2, 3)
        put(7)

    def relay_third():
        got(13)
        put(15)
        got(14)
        put(16)

    @core(0)
    def _():
        begin()
        relay_first()

    weights.got(0, key_slice)
    weights.got(1, value_slice)
    weights.put(2, slice_of(0, 0), slice_of(0, 0), me.zp)
    weights.put(3, slice_of(0, 0), slice_of(0, 0), me.zm)
    weights.put(6, slice_of(0, 0), slice_of(0, 0), me.sib)

    @core(0)
    def _():
        relay_second()
        relay_third()
        pl.semaphore_signal(gate, inc=1, device_id=me.sib, device_id_type=MESH)

    weights.got(2, slice_of(-1, 0))
    weights.put(4, slice_of(-1, 0, 0, 256), slice_of(-1, 0, 0, 256), me.zp)
    weights.put(7, slice_of(-1, 0), slice_of(-1, 0), me.sib)
    weights.got(3, slice_of(1, 0))
    weights.put(5, slice_of(1, 0, 256, 256), slice_of(1, 0, 256, 256), me.zm)
    weights.put(8, slice_of(1, 0), slice_of(1, 0), me.sib)

    @core(1)
    def _():
        pl.semaphore_wait(gate, 1)
        begin()

    weights.got(4, slice_of(2, 0, 0, 256))
    weights.got(5, slice_of(2, 0, 256, 256))
    weights.put(9, slice_of(2, 0), slice_of(2, 0), me.sib)
    load_k.wait()
    load_v.wait()

    @core(1)
    def _():
        relay_first()

    def project(row, count, matrix, out):
        block = at(row, count)
        out[block, :] = jnp.dot(
            xg[block, :], matrix[...], preferred_element_type=F32
        ).astype(BF16)

    def give_heads(i, row, count):
        project(row, count, wp, kvs)
        heads.put(
            i,
            lambda: kvs.at[at(row, count)],
            lambda: kv.at[at(row + 1024, count)],
            me.pair,
        )

    got(4)
    project(me.column(0), 256, w, kv)
    for i, dz in enumerate((0, -1, 1, 2)):
        weights.got(6 + i, slice_of(dz, 1))
    give_heads(0, me.column(0), 256)

    @core(1)
    def _():
        relay_second()
        relay_third()

    got(5)
    give_heads(1, me.column(-1), 256)
    project(me.column(-1), 256, w, kv)
    got(6)
    give_heads(2, me.column(1), 256)
    project(me.column(1), 256, w, kv)
    got(11, 12)
    far = me.block(2, 0)
    give_heads(3, far, 128)
    project(far, 128, w, kv)
    got(15, 16, 7)
    last = me.block(2, 1)
    give_heads(4, last, 128)
    project(last, 128, w, kv)
    weights.got(10, whole(qr))
    weights.got(11, whole(gr))
    given = ((me.column(0), 256), (me.column(-1), 256), (me.column(1), 256), (far, 128), (last, 128))
    for i, (start, count) in enumerate(given):
        heads.got(i, lambda: kv.at[at(start + 1024, count)])


    length = len_ref[me.position]
    lane = lax.broadcasted_iota(jnp.int32, (1, 2048), 1)
    number = (lane % 1024) // ROWS
    group = (me.group + lane // 1024) % 2
    row_y = group + (number % 2) * (3 - 2 * group)
    visible = ((number // 2) * 4 + row_y) * ROWS + lane % ROWS < length
    scale = HD**-0.5

    def attend(i, _):
        here = at(i * 128, 128)
        scores = lax.dot_general(qr[here, :], kv[:, 0:HD], NT, preferred_element_type=F32)
        scores = jnp.where(visible, scores * scale, NEG_FILL)
        top = jnp.max(scores, axis=-1, keepdims=True)
        exponent = jnp.exp(scores - top)
        total = jnp.sum(exponent, axis=-1, keepdims=True)
        probs = exponent * (1.0 / total)
        weights16 = probs.astype(BF16)
        pbuf[here, :] = weights16
        att[here, :] = jnp.dot(
            weights16, kv[:, HD : 2 * HD], preferred_element_type=F32
        ).astype(BF16)
        grad_probs = lax.dot_general(
            gr[here, :], kv[:, HD : 2 * HD], NT, preferred_element_type=F32
        )
        inner = jnp.sum(probs * grad_probs, axis=-1, keepdims=True)
        grad_scores = (probs * (grad_probs - inner) * scale).astype(BF16)
        sbuf[here, :] = grad_scores
        dq[here, :] = jnp.dot(
            grad_scores, kv[:, 0:HD], preferred_element_type=F32
        ).astype(BF16)
        return 0

    lax.fori_loop(0, TGT // 128, attend, 0)

    def head_grads(start):
        here = at(start, 256)
        kvg[here, 0:HD] = lax.dot_general(
            sbuf[:, here], qr[...], TN, preferred_element_type=F32
        ).astype(BF16)
        kvg[here, HD : 2 * HD] = lax.dot_general(
            pbuf[:, here], gr[...], TN, preferred_element_type=F32
        ).astype(BF16)

    def pair_rows(dx):
        return lambda: kvp.at[at(me.column(dx), 256)]

    for i, dx in enumerate(ORDER):
        theirs = me.column(dx) + 1024
        head_grads(theirs)
        heads.put(5 + i, lambda start=theirs: kvg.at[at(start, 256)], pair_rows(dx), me.pair)
    heads.put(9, whole(att), whole(att_out), me.across)
    heads.put(10, whole(dq), whole(dq_out), me.across)
    for dx in ORDER:
        head_grads(me.column(dx))
    kt[0] = kvg[0:1024, :].T


    def row_terms(dx):
        here = at(me.column(dx), 256)
        heads.got(5 + ORDER.index(dx), pair_rows(dx))

        def tile(n, _):
            cols = at(n * 512, 512)
            total = lax.dot_general(kvg[here, :], w[cols, :], NT, preferred_element_type=F32)
            total += lax.dot_general(kvp[here, :], wp[cols, :], NT, preferred_element_type=F32)
            r[here, cols] = total.astype(BF16)
            return 0

        lax.fori_loop(0, D // 512, tile, 0)

    def add(row, cols, source, first=0):
        lo, hi = cols[0], cols[0] + cols[1]

        def some(i, _):
            here = at(row + i * 16, 16)
            came = source()[at(i * 16, 16), first : first + cols[1]]
            r[here, lo:hi] = (r[here, lo:hi].astype(F32) + came.astype(F32)).astype(BF16)
            return 0

        lax.fori_loop(0, ROWS // 16, some, 0)

    def y_top(dx):
        i = ORDER.index(dx)
        back.put(i, part(r, lambda: me.block(dx, 1), TOP), lambda: yt.at[i], me.yn)

    def y_top_add(dx):
        i = ORDER.index(dx)
        back.got(i, lambda: yt.at[i])
        add(me.block(dx, 0), TOP, lambda: yt.at[i])

    ring_of = {
        "top": (0, TOP, TOP_A, TOP_B, 4, lambda: ta, lambda j: tc.at[j]),
        "low0": (0, LOW, LOW_A, LOW_B, 8, lambda: la.at[0], lambda j: lc.at[j]),
        "low1": (1, LOW, LOW_A, LOW_B, 12, lambda: la.at[1], lambda j: lc.at[2 + j]),
    }

    def ring_first(name):
        group_, _, a, b, i, halves, _ = ring_of[name]
        size = a[1]
        back.put(i, part(r, lambda: me.block(2, group_), a), lambda: halves().at[:, 0:size], me.xp)
        back.put(
            i + 1, part(r, lambda: me.block(2, group_), b), lambda: halves().at[:, size : 2 * size], me.xm
        )

    def ring_second(name):
        group_, cols, a, b, i, halves, ends = ring_of[name]
        size = a[1]
        back.got(i, lambda: halves().at[:, 0:size])
        add(me.block(1, group_), a, halves)
        back.put(i + 2, part(r, lambda: me.block(1, group_), cols), lambda: ends(0), me.xp)
        back.got(i + 1, lambda: halves().at[:, size : 2 * size])
        add(me.block(-1, group_), b, halves, size)
        back.put(i + 3, part(r, lambda: me.block(-1, group_), cols), lambda: ends(1), me.xm)

    def ring_wait(name):
        _, _, _, _, i, _, ends = ring_of[name]
        back.got(i + 2, lambda: ends(0))
        back.got(i + 3, lambda: ends(1))


    def grad_term(h, dz, sibling):
        z = (me.z + dz) % 4
        c = 1 - me.core if sibling else me.core
        return jnp.dot(kt[h], xg[:, at((z * 2 + c) * 512, 512)], preferred_element_type=F32)

    staged = (pbuf, sbuf)

    def near_put(h, n):
        src = lambda: staged[h].at[:, n * 512 : (n + 1) * 512]
        staged[h][:, n * 512 : (n + 1) * 512] = grad_term(h, ORDER[n], 1).astype(BF16)
        near.put(h * 4 + n, src, lambda: gb.at[h * 4 + n], me.sib)

    def near_add(h, n):
        term = grad_term(h, ORDER[n], 0)
        near.got(h * 4 + n, lambda: gb.at[h * 4 + n])
        gb[h * 4 + n] = (gb[h * 4 + n].astype(F32) + term).astype(BF16)

    def z_first(h):
        rings.put(h * 6, lambda: gb.at[h * 4, 0:256], lambda: zb.at[h, 0:256], me.zp)
        rings.put(h * 6 + 1, lambda: gb.at[h * 4, 256:512], lambda: zb.at[h, 256:512], me.zm)

    def z_second(h):
        rings.got(h * 6, lambda: zb.at[h, 0:256])
        gb[h * 4 + 1, 0:256] = (
            gb[h * 4 + 1, 0:256].astype(F32) + zb[h, 0:256].astype(F32)
        ).astype(BF16)
        rings.got(h * 6 + 1, lambda: zb.at[h, 256:512])
        gb[h * 4 + 2, 256:512] = (
            gb[h * 4 + 2, 256:512].astype(F32) + zb[h, 256:512].astype(F32)
        ).astype(BF16)
        for j in range(2):
            here = slice(j * 256, j * 256 + 256)
            rings.put(
                h * 6 + 2 + j,
                lambda here=here: gb.at[h * 4 + 1, here],
                lambda j=j: zb.at[h, 512 + j * 256 : 768 + j * 256],
                me.zp,
            )
            rings.put(
                h * 6 + 4 + j,
                lambda here=here: gb.at[h * 4 + 2, here],
                lambda j=j: zb.at[h, 1024 + j * 256 : 1280 + j * 256],
                me.zm,
            )

    def z_sum(h, j):
        first, second = 512 + j * 256, 1024 + j * 256
        rings.got(h * 6 + 2 + j, lambda: zb.at[h, first : first + 256])
        rings.got(h * 6 + 4 + j, lambda: zb.at[h, second : second + 256])
        return (
            gb[h * 4 + 3, j * 256 : j * 256 + 256].astype(F32)
            + zb[h, first : first + 256].astype(F32)
            + zb[h, second : second + 256].astype(F32)
        )

    for n in range(4):
        near_put(0, n)

    @core(1)
    def _():
        near_add(0, 0)
        z_first(0)

    row_terms(2)
    y_top(2)
    ring_first("low1")
    ring_first("low0")

    @core(1)
    def _():
        near_add(0, 1)
        near_add(0, 2)
        z_second(0)

    row_terms(1)
    y_top(1)
    row_terms(-1)
    y_top(-1)
    ring_second("low1")
    y_top_add(2)
    ring_first("top")
    row_terms(0)
    y_top(0)
    kt[1] = kvp[...].T
    for n in range(4):
        near_put(1, n)
    ring_second("low0")

    @core(0)
    def _():
        near_add(0, 0)
        z_first(0)
        near_add(0, 1)
        near_add(0, 2)
        z_second(0)

    near_add(1, 0)
    z_first(1)
    near_add(1, 1)
    near_add(1, 2)
    y_top_add(1)
    y_top_add(-1)
    ring_second("top")
    z_second(1)
    ring_wait("low1")
    add(me.block(0, 1), LOW, lambda: lc.at[2])
    add(me.block(0, 1), LOW, lambda: lc.at[3])
    back.put(16, part(r, lambda: me.block(0, 1), LOW), whole(yl), me.yn)
    near_add(0, 3)
    near_add(1, 3)
    for j in range(2):
        ps[j] = z_sum(1, j).astype(BF16)
        heads.put(11 + j, lambda j=j: ps.at[j], lambda j=j: pb.at[j], me.pair)
    for j in range(2):
        here = slice(j * 256, j * 256 + 256)
        col_grad[here, :] = z_sum(0, j)
    for j in range(2):
        here = slice(j * 256, j * 256 + 256)
        heads.got(11 + j, lambda: pb.at[j])
        col_grad[here, :] += pb[j].astype(F32)

    back.got(3, lambda: yt.at[3])
    ring_wait("low0")
    ring_wait("top")
    back.got(16, whole(yl))

    def finish(cols, *sources):
        lo, hi = cols[0], cols[0] + cols[1]

        def some(i, _):
            grad = r[at(own + i * 16, 16), lo:hi].astype(F32)
            for source in sources:
                grad += source()[at(i * 16, 16), :].astype(F32)
            row_grad[at(i * 16, 16), lo:hi] = grad.astype(BF16)
            return 0

        lax.fori_loop(0, ROWS // 16, some, 0)

    finish(TOP, lambda: tc.at[0], lambda: tc.at[1], lambda: yt.at[3])
    finish(LOW, lambda: lc.at[0], lambda: lc.at[1], whole(yl))

    heads.got(9, whole(att_out))
    heads.got(10, whole(dq_out))
    for wires in (rows, weights, heads, back, near, rings):
        wires.close()


def results_kernel(enc, gain, row_grad, col_grad, att_in, dq_in, enc_grad, kg, vg, att, dq):
    wide = enc[...].astype(F32)
    factor = lax.rsqrt(jnp.mean(wide * wide, axis=-1, keepdims=True) + EPS)
    scaled = row_grad[...].astype(F32) * gain[...]
    inner = jnp.mean(scaled * wide, axis=-1, keepdims=True)
    enc_grad[...] = (factor * scaled - wide * (factor * factor * factor * inner)).astype(BF16)
    kg[...] = col_grad[0:HD, :].T
    vg[...] = col_grad[HD : 2 * HD, :].T
    att[...] = att_in[...]
    dq[...] = dq_in[...]


def on_device(enc_states, enc_gain, key_weight, value_weight, queries, out_grad, lengths):
    enc = enc_states[0]
    gain = enc_gain.reshape(1, D)
    vmem = pl.BlockSpec(memory_space=pltpu.VMEM)
    far = pl.BlockSpec(memory_space=pl.ANY)
    dma = pltpu.SemaphoreType.DMA
    shape = jax.ShapeDtypeStruct
    low = D - CUT

    row_grad, col_grad, att, dq = pl.pallas_call(
        kernel,
        out_shape=(
            shape((ROWS, D), BF16),
            shape((2 * HD, 512), F32),
            shape((TGT, HD), BF16),
            shape((TGT, HD), BF16),
        ),
        in_specs=[pl.BlockSpec(memory_space=pltpu.SMEM), vmem, vmem, far, far, far, far],
        out_specs=(vmem, vmem, far, far),
        scratch_shapes=[
            pltpu.VMEM((1024, D), BF16),
            pltpu.VMEM((D, 2 * HD), BF16),
            pltpu.VMEM((D, 2 * HD), BF16),
            pltpu.VMEM((2048, 2 * HD), BF16),
            pltpu.VMEM((1024, 2 * HD), BF16),
            pltpu.VMEM((TGT, HD), BF16),
            pltpu.VMEM((TGT, HD), BF16),
            pltpu.VMEM((TGT, 2048), BF16),
            pltpu.VMEM((TGT, 2048), BF16),
            pltpu.VMEM((TGT, HD), BF16),
            pltpu.VMEM((TGT, HD), BF16),
            pltpu.VMEM((2048, 2 * HD), BF16),
            pltpu.VMEM((1024, 2 * HD), BF16),
            pltpu.VMEM((2, 2 * HD, 1024), BF16),
            pltpu.VMEM((1024, D), BF16),
            pltpu.VMEM((4, ROWS, CUT), BF16),
            pltpu.VMEM((ROWS, CUT), BF16),
            pltpu.VMEM((2, ROWS, CUT), BF16),
            pltpu.VMEM((2, ROWS, low), BF16),
            pltpu.VMEM((4, ROWS, low), BF16),
            pltpu.VMEM((ROWS, low), BF16),
            pltpu.VMEM((8, 512, 512), BF16),
            pltpu.VMEM((2, 1536, 512), BF16),
            pltpu.VMEM((2, 256, 512), BF16),
            pltpu.VMEM((2, 256, 512), BF16),
            dma((17,)),
            dma((17,)),
            dma((12,)),
            dma((12,)),
            dma((13,)),
            dma((13,)),
            dma((17,)),
            dma((17,)),
            dma((8,)),
            dma((8,)),
            dma((12,)),
            dma((12,)),
            dma((2,)),
            pltpu.SemaphoreType.REGULAR,
        ],
        compiler_params=pltpu.CompilerParams(
            collective_id=0, has_side_effects=True, vmem_limit_bytes=VMEM_BYTES
        ),
        name="gather_attend_scatter",
    )(lengths, enc, gain, key_weight, value_weight, queries[0], out_grad[0])

    def rows_of(count, width):
        return pl.BlockSpec((count, width), lambda i: (i, 0))

    enc_grad, kg, vg, att, dq = pl.pallas_call(
        results_kernel,
        grid=(4,),
        out_shape=(
            shape((ROWS, D), BF16),
            shape((512, HD), F32),
            shape((512, HD), F32),
            shape((TGT, HD), BF16),
            shape((TGT, HD), BF16),
        ),
        in_specs=[
            rows_of(32, D),
            pl.BlockSpec((1, D), lambda i: (0, 0)),
            rows_of(32, D),
            pl.BlockSpec((2 * HD, 128), lambda i: (0, i)),
            rows_of(128, HD),
            rows_of(128, HD),
        ],
        out_specs=(
            rows_of(32, D),
            rows_of(128, HD),
            rows_of(128, HD),
            rows_of(128, HD),
            rows_of(128, HD),
        ),
        name="results",
    )(enc, gain, row_grad, col_grad, att, dq)
    return (att[None], enc_grad[None], kg, vg, dq[None])


def solution(mesh):
    placed = (
        P(("section", "dp"), "seq", None),
        P(),
        P(None, "seq"),
        P(None, "seq"),
        P(("section", "dp"), None, "seq"),
        P(("section", "dp"), None, "seq"),
        P(),
    )
    return jax.shard_map(
        on_device,
        mesh=mesh,
        in_specs=placed,
        out_specs=(
            P(("section", "dp"), None, "seq"),
            P(("section", "dp"), "seq", None),
            P(("section", "dp"), "seq"),
            P(("section", "dp"), "seq"),
            P(("section", "dp"), None, "seq"),
        ),
        check_vma=False,
    )
```

time: 363 us -> 147 us (0.40)
  waiting for transfers between devices: 266 us -> 0 us
  Pallas kernels: 0 us -> 146 us
  matrix products: 54.7 us -> 0 us
  between operations: 14 us -> 0.82 us
  other arithmetic: 11 us -> 0 us
  local copies, waits for them, and re-layouts: 9.37 us -> 0 us
  starting transfers between devices: 7.45 us -> 0 us
    pallas_call x0 -> x2, Pallas kernels: none -> 146 us  [the longest x1 141 us: on_device(): pl.pallas_call(kernel, out_shape=(shape((ROWS, D), BF16), shape((2 * HD,...]
    reduce_scatter x2 -> x0, waiting for transfers between devices: 133 us -> none  [the longest x1 95.6 us: on_device(): lax.psum_scatter(lax.dot_general(kv_grads, projection, (((1,), (1,)), (()...]
    all_gather x1 -> x0, waiting for transfers between devices: 109 us -> none  [on_device(): gathered = lax.all_gather(partner_rows, 'seq', axis=0, tiled=True)]
    dot_general x9 -> x0, matrix products: 54.7 us -> none  [the longest x1 14.6 us: on_device(): lax.dot_general(kv_grads, projection, (((1,), (1,)), ((), ())), preferred...]
    ppermute x2 -> x0, waiting for transfers between devices: 22.9 us -> none  [partner_2(): return lax.ppermute(value, axis, pairs)]
    ppermute x2 -> x0, starting transfers between devices: 7.33 us -> none  [partner_2(): return lax.ppermute(value, axis, pairs)]
    unnamed x29 -> x0, local copies, waits for them, and re-layouts: 5.2 us -> none
    reduce_sum x3 -> x0, other arithmetic: 4.34 us -> none  [the longest x1 1.67 us: normalize(): jnp.mean(wide_rows * wide_rows, axis=-1, keepdims=True) + EPS]
  transfers between devices with their start and end apart: 5 -> 0, of which waited for: 4 -> 0; matrix products, arithmetic and copies ran while one was open for 8% -> 0% of each run, Pallas kernels for 0% -> 0%
where the time goes in v2:
time: 147 us
  Pallas kernels  146 us (99%)
    pallas_call x1, Pallas kernels, on_device(): pl.pallas_call(kernel, out_shape=(shape((ROWS, D), BF16), shape((2 * HD,...  141 us
    pallas_call x1, Pallas kernels, on_device(): pl.pallas_call(results_kernel, grid=(4,), out_shape=(shape((ROWS, D), BF1...  4.65 us

profile of v2, /device:TPU:1, one launch (start us, length us, event | category | flops | bytes accessed | tf_op | source)
XLA Modules:
  0.0 146.9 jit_solution(15595324597415459526)
XLA Ops:
  0.6 141.4 %gather_attend_scatter.1 = (bf16[128,4096]{1,0:T(8,128)(2,1)}, f32[512,512]{1,0:T(8,128)}, bf16[512,256]{1,0:T(8,128)(2,1)}, bf16[512,256]{1,0:T(8,128)(2,1)}) custom-call(s32[8]{0:T(128)} %len_ref.1, bf16[128,4096]{1,0:T(8,128)(2,1)} %bitcast.7, f32[1,4096]{1,0:T(1,128)} %bitcast.11, bf16[4096,256]{1,0:T(8,128)(2,1)} %kw.1, bf16[4096,256]{1,0:T(8,128)(2,1)} %vw.1, ...), custom_call_target="tpu_custom_call" | custom-call | tf_op jit(solution)/shard_map/gather_attend_scatter/pallas_call | solution.py:607
  142.1 4.6 %results.1 = (bf16[128,4096]{1,0:T(8,128)(2,1)}, f32[512,256]{1,0:T(8,128)}, f32[512,256]{1,0:T(8,128)}, bf16[512,256]{1,0:T(8,128)(2,1)}, bf16[512,256]{1,0:T(8,128)(2,1)}) custom-call(bf16[128,4096]{1,0:T(8,128)(2,1)} %bitcast.8, f32[1,4096]{1,0:T(1,128)} %bitcast.12, bf16[128,4096]{1,0:T(8,128)(2,1)} %get-tuple-element.14.row_grad, ...), custom_call_target="tpu_custom_call" | custom-call | tf_op jit(solution)/shard_map/results/pallas_call | solution.py:667

commit v3 on v2

v3 whole, which is shorter than its diff:
```python
import jax
import jax.numpy as jnp
from jax import lax
from jax.experimental import pallas as pl
from jax.experimental.pallas import tpu as pltpu
from jax.sharding import PartitionSpec as P

D = 4096
HD = 256
TGT = 512
ROWS = 128
EPS = 1e-06
NEG_FILL = -1e30
MESH = pl.DeviceIdType.MESH
F32 = jnp.float32
BF16 = jnp.bfloat16
VMEM_BYTES = 62 * 1024 * 1024
NT = (((1,), (1,)), ((), ()))
TN = (((0,), (0,)), ((), ()))
CUT = 1792
TOP = (0, CUT)
TOP_A, TOP_B = (0, CUT // 2), (CUT // 2, CUT // 2)
LOW = (CUT, D - CUT)
LOW_A, LOW_B = (CUT, (D - CUT) // 2), (CUT + (D - CUT) // 2, (D - CUT) // 2)


class Place:
    def __init__(self):
        section, dp, seq = (lax.axis_index(a) for a in ("section", "dp", "seq"))
        self.x, self.y = seq // 4, seq % 4
        self.core = dp % 2
        self.z = section * 2 + dp // 2
        self.position = section * 4 + dp
        x, y, z, core = self.x, self.y, self.z, self.core
        self.ky = y // 2
        self.group = (y % 2 + y // 2) % 2
        self.xp = (section, dp, ((x + 1) % 4) * 4 + y)
        self.xm = (section, dp, ((x + 3) % 4) * 4 + y)
        self.yn = (section, dp, x * 4 + 3 - y)
        self.pair = (section, dp, x * 4 + y + 1 - 2 * (y % 2))
        self.sib = (section, dp + 1 - 2 * core, seq)
        zp, zm = (z + 1) % 4, (z + 3) % 4
        self.zp = (zp // 2, (zp % 2) * 2 + core, seq)
        self.zm = (zm // 2, (zm % 2) * 2 + core, seq)
        self.across = (1 - section, dp, seq)

    def column(self, dx):
        return ((self.x + dx) % 4) * 2 * ROWS

    def block(self, dx, w):
        return self.column(dx) + (self.ky if w == 0 else 1 - self.ky) * ROWS

    def enter(self, meanwhile):
        everyone = (
            self.xp,
            self.xm,
            self.yn,
            self.pair,
            self.sib,
            self.zp,
            self.zm,
            self.across,
        )
        barrier = pltpu.get_barrier_semaphore()
        for device in everyone:
            pl.semaphore_signal(barrier, inc=1, device_id=device, device_id_type=MESH)
        meanwhile()
        pl.semaphore_wait(barrier, len(everyone))


def at(start, size, unit=None):
    return pl.ds(pl.multiple_of(start, unit or min(size, 256)), size)


class Wires:
    def __init__(self, send, recv, home):
        self.send, self.recv, self.home = send, recv, home
        self.open = {}

    def copy(self, i, src, dst, device):
        return pltpu.make_async_remote_copy(
            src_ref=src,
            dst_ref=dst,
            send_sem=self.send.at[i],
            recv_sem=self.recv.at[i],
            device_id=device,
            device_id_type=MESH,
        )

    def put(self, i, src, dst, device):
        self.copy(i, src(), dst(), device).start()
        self.open[i] = src

    def got(self, i, dst):
        self.copy(i, dst(), dst(), self.home).wait_recv()

    def close(self):
        for i, src in self.open.items():
            self.copy(i, src(), src(), self.home).wait_send()


GATHER_GOT = (
    (-1, 0, TOP),
    (1, 0, TOP),
    (2, 0, TOP_A),
    (2, 0, TOP_B),
    (0, 1, TOP),
    (-1, 1, TOP),
    (1, 1, TOP),
    (2, 1, TOP),
    (0, 1, LOW),
    (-1, 0, LOW),
    (1, 0, LOW),
    (2, 0, LOW_A),
    (2, 0, LOW_B),
    (-1, 1, LOW),
    (1, 1, LOW),
    (2, 1, LOW_A),
    (2, 1, LOW_B),
)
GATHER_PUT = (
    (0, 0, TOP, "xp"),
    (0, 0, TOP, "xm"),
    (-1, 0, TOP_A, "xp"),
    (1, 0, TOP_B, "xm"),
    (0, 0, TOP, "yn"),
    (-1, 0, TOP, "yn"),
    (1, 0, TOP, "yn"),
    (2, 0, TOP, "yn"),
    (0, 0, LOW, "yn"),
    (0, 0, LOW, "xp"),
    (0, 0, LOW, "xm"),
    (-1, 0, LOW_A, "xp"),
    (1, 0, LOW_B, "xm"),
    (0, 1, LOW, "xp"),
    (0, 1, LOW, "xm"),
    (-1, 1, LOW_A, "xp"),
    (1, 1, LOW_B, "xm"),
)
ORDER = (2, 1, -1, 0)
STEPS = (
    "begin@0", "r1@0", "r8@0", "w1K", "w1V", "r0@0", "r10@0", "r9@0", "r13@0", "r23@0", "w2aK",
    "r14@0", "w2bK", "gate@0", "w2aV", "w2bV", "begin@1", "w3K", "w3V", "wallK", "r8@1",
    "wallV", "r0@1", "r1@1", "q", "gV0", "r9@1", "gK0", "o0", "r13@1", "r10@1", "gV-1", "r23@1",
    "r14@1", "gK-1", "gV1", "o1", "gK1", "gate3@1", "gVfar", "ofar", "g", "gVlast", "gKlast",
    "gKfar", "o-1", "olast", "att", "ao", "hgpA", "hgo1", "hgo0", "hgo3", "hgo2", "hgpB",
    "hgp1", "hgp2", "kt0", "hgp3", "np00", "na00@1", "na02@1", "RA", "na01@1", "np02", "RB",
    "zD0@1", "np01", "zC0@1", "R1", "low1C", "R-1", "low1D", "na00@0", "kt1", "np10", "np11",
    "ya2", "R0", "na02@0", "na01@0", "np12", "zD0@0", "zC0@0", "low0D", "low0C", "np03", "ya1",
    "np13", "na10", "yl", "na11", "na12", "na03", "ya-1", "topC", "zs00", "zD1", "zC1", "na13",
    "topD", "zs10", "zs11", "zs01", "pf0", "fin", "pf1",
)


def kernel(
    len_ref, enc, gain, kw, vw, q, g,
    row_grad, col_grad, att_out, dq_out,
    xg, w, wp, kv, kvs, qr, gr, pbuf, sbuf, att, dq, kvg, kvp, kt,
    r, yt, ta, tc, la, lc, yl, gb, zb, ps, pb,
    xs, xr, ws, wr, hs, hr, bs, br, ns, nr, zs, zr, loc, gates,
):
    me = Place()
    load_k = pltpu.make_async_copy(kw, w.at[:, 0:HD], loc.at[0])
    load_v = pltpu.make_async_copy(vw, w.at[:, HD : 2 * HD], loc.at[1])
    load_k.start()
    load_v.start()
    own = me.block(0, 0)

    def norm():
        def some(i, _):
            wide = enc[at(i * 32, 32), :].astype(F32)
            factor = lax.rsqrt(jnp.mean(wide * wide, axis=-1, keepdims=True) + EPS)
            xg[at(own + i * 32, 32), :] = (wide * factor * gain[...]).astype(BF16)
            return 0

        lax.fori_loop(0, ROWS // 32, some, 0)

    me.enter(norm)

    rows = Wires(xs, xr, me.xp)
    weights = Wires(ws, wr, me.zp)
    heads = Wires(hs, hr, me.pair)
    back = Wires(bs, br, me.xp)
    near = Wires(ns, nr, me.sib)
    rings = Wires(zs, zr, me.zp)
    tasks = {}

    def whole(ref):
        return lambda: ref

    def part(ref, row, cols):
        return lambda: ref.at[at(row(), ROWS), cols[0] : cols[0] + cols[1]]


    def piece(spec):
        return part(xg, lambda: me.block(spec[0], spec[1]), spec[2])

    def put(*ids):
        for i in ids:
            spec = GATHER_PUT[i]
            rows.put(i, piece(spec), piece(spec), getattr(me, spec[3]))

    def got(*ids):
        for i in ids:
            rows.got(i, piece(GATHER_GOT[i]))

    def begin():
        @pl.when(me.core == 1)
        def _():
            pl.semaphore_wait(gates.at[0], 1)

        put(0, 1, 8, 9, 10, 4)

    def relay(waits, sends):
        def run():
            got(*waits)
            put(*sends)

        return run

    def signal(i):
        return lambda: pl.semaphore_signal(
            gates.at[i], inc=1, device_id=me.sib, device_id_type=MESH
        )

    tasks["begin"] = begin
    tasks["r8"] = relay((8,), (13, 14))
    tasks["r0"] = relay((0,), (2, 5))
    tasks["r1"] = relay((1,), (3, 6))
    tasks["r9"] = relay((9,), (11,))
    tasks["r10"] = relay((10,), (12,))
    tasks["r23"] = relay((2, 3), (7,))
    tasks["r13"] = relay((13,), (15,))
    tasks["r14"] = relay((14,), (16,))
    tasks["gate"] = signal(0)
    tasks["gate3"] = signal(1)

    for k, kind in enumerate("KV"):

        def one(base, cols, kind):
            def slice_of(dz, sibling, first=0, count=512):
                z = (me.z + dz) % 4
                c = 1 - me.core if sibling else me.core
                start = (z * 2 + c) * 512 + first
                return lambda: wp.at[at(start, count), cols]

            mine, back_, ahead = (slice_of(dz, 0) for dz in (0, -1, 1))
            far, far_a, far_b = (
                slice_of(2, 0),
                slice_of(2, 0, 0, 256),
                slice_of(2, 0, 256, 256),
            )
            others = [slice_of(dz, 1) for dz in (0, -1, 1, 2)]
            back_a, ahead_b = slice_of(-1, 0, 0, 256), slice_of(1, 0, 256, 256)
            source = (kw, vw)[k]
            row = me.position * 512
            weights.put(base, lambda: source.at[at(row, 512)], mine, me.pair)

            def w1():
                weights.got(base, mine)
                weights.put(base + 1, mine, mine, me.zp)
                weights.put(base + 2, mine, mine, me.zm)
                weights.put(base + 5, mine, mine, me.sib)
                if kind == "V":
                    load_k.wait()
                    load_v.wait()

            def w2a():
                weights.got(base + 1, back_)
                weights.put(base + 3, back_a, back_a, me.zp)
                weights.put(base + 6, back_, back_, me.sib)

            def w2b():
                weights.got(base + 2, ahead)
                weights.put(base + 4, ahead_b, ahead_b, me.zm)
                weights.put(base + 7, ahead, ahead, me.sib)

            def w3():
                weights.got(base + 3, far_a)
                weights.got(base + 4, far_b)
                weights.put(base + 8, far, far, me.sib)

            def wall():
                for i in range(4):
                    weights.got(base + 5 + i, others[i])

            tasks["w1" + kind] = w1
            tasks["w2a" + kind] = w2a
            tasks["w2b" + kind] = w2b
            tasks["w3" + kind] = w3
            tasks["wall" + kind] = wall

        one(9 * k, slice(k * HD, k * HD + HD), kind)

    tasks["q"] = lambda: weights.put(18, whole(q), whole(qr), me.across)
    tasks["g"] = lambda: weights.put(19, whole(g), whole(gr), me.across)

    columns = {
        "0": (lambda: me.column(0), 256, (4, 8)),
        "-1": (lambda: me.column(-1), 256, (0, 9, 5, 13)),
        "1": (lambda: me.column(1), 256, (1, 10, 6, 14)),
        "far": (lambda: me.block(2, 0), 128, (2, 3, 11, 12)),
        "last": (lambda: me.block(2, 1), 128, (7, 15, 16)),
    }
    relayed = (8, 0, 1, 9, 10, 2, 3, 13, 14)
    seen = set()

    def project(name, kind):
        start, count, needed = columns[name]
        got(*(i for i in needed if i not in relayed and i not in seen))
        seen.update(needed)
        here = at(start(), count)
        if kind == "o":
            kv[here, :] = jnp.dot(xg[here, :], w[...], preferred_element_type=F32).astype(BF16)
            return
        k = "KV".index(kind)
        cols = slice(k * HD, k * HD + HD)
        kvs[here, cols] = jnp.dot(
            xg[here, :], wp[:, cols], preferred_element_type=F32
        ).astype(BF16)
        heads.put(
            k * 5 + list(columns).index(name),
            lambda: kvs.at[at(start(), count), cols],
            lambda: kv.at[at(start() + 1024, count), cols],
            me.pair,
        )


    def attention():
        for k in range(2):
            for i, (start, count, _) in enumerate(columns.values()):
                heads.got(
                    k * 5 + i,
                    lambda: kv.at[at(start() + 1024, count), k * HD : k * HD + HD],
                )
        weights.got(18, whole(qr))
        weights.got(19, whole(gr))
        length = len_ref[me.position]
        lane = lax.broadcasted_iota(jnp.int32, (1, 2048), 1)
        number = (lane % 1024) // ROWS
        group = (me.group + lane // 1024) % 2
        row_y = group + (number % 2) * (3 - 2 * group)
        visible = ((number // 2) * 4 + row_y) * ROWS + lane % ROWS < length
        scale = HD**-0.5

        def attend(i, _):
            here = at(i * 256, 256)
            scores = lax.dot_general(qr[here, :], kv[:, 0:HD], NT, preferred_element_type=F32)
            scores = jnp.where(visible, scores * scale, NEG_FILL)
            top = jnp.max(scores, axis=-1, keepdims=True)
            exponent = jnp.exp(scores - top)
            total = jnp.sum(exponent, axis=-1, keepdims=True)
            probs = exponent * (1.0 / total)
            weights16 = probs.astype(BF16)
            pbuf[here, :] = weights16
            att[here, :] = jnp.dot(
                weights16, kv[:, HD : 2 * HD], preferred_element_type=F32
            ).astype(BF16)
            grad_probs = lax.dot_general(
                gr[here, :], kv[:, HD : 2 * HD], NT, preferred_element_type=F32
            )
            inner = jnp.sum(probs * grad_probs, axis=-1, keepdims=True)
            grad_scores = (probs * (grad_probs - inner) * scale).astype(BF16)
            sbuf[here, :] = grad_scores
            dq[here, :] = jnp.dot(
                grad_scores, kv[:, 0:HD], preferred_element_type=F32
            ).astype(BF16)
            return 0

        lax.fori_loop(0, TGT // 256, attend, 0, unroll=True)

    tasks["att"] = attention

    def head_grads(start, count):
        here = at(start, count)
        kvg[here, 0:HD] = lax.dot_general(
            sbuf[:, here], qr[...], TN, preferred_element_type=F32
        ).astype(BF16)
        kvg[here, HD : 2 * HD] = lax.dot_general(
            pbuf[:, here], gr[...], TN, preferred_element_type=F32
        ).astype(BF16)

    given = {
        "A": (lambda: me.block(2, 1), 128),
        "B": (lambda: me.block(2, 0), 128),
        "1": (lambda: me.column(1), 256),
        "2": (lambda: me.column(-1), 256),
        "3": (lambda: me.column(0), 256),
    }

    def give_grads(name):
        start, count = given[name]

        def run():
            if name == "1":

                @pl.when(me.core == 0)
                def _():
                    pl.semaphore_wait(gates.at[1], 1)

            head_grads(start() + 1024, count)
            heads.put(
                10 + list(given).index(name),
                lambda: kvg.at[at(start() + 1024, count)],
                lambda: kvp.at[at(start(), count)],
                me.pair,
            )

        return run

    for name in given:
        tasks["hgp" + name] = give_grads(name)
    for i, dx in enumerate(ORDER):
        tasks["hgo%d" % i] = lambda dx=dx: head_grads(me.column(dx), 256)

    def results_back():
        heads.put(15, whole(att), whole(att_out), me.across)
        heads.put(16, whole(dq), whole(dq_out), me.across)

    tasks["ao"] = results_back

    def turn(h):
        kt[h] = (kvg[0:1024, :] if h == 0 else kvp[...]).T


    def got_grads(name):
        if name not in seen:
            seen.add(name)
            start, count = given[name]
            heads.got(10 + list(given).index(name), lambda: kvp.at[at(start(), count)])

    def row_terms(name):
        got_grads(name)
        start, count = given[name]
        here = at(start(), count)

        def tile(n, _):
            cols = at(n * 512, 512)
            total = lax.dot_general(kvg[here, :], w[cols, :], NT, preferred_element_type=F32)
            total += lax.dot_general(kvp[here, :], wp[cols, :], NT, preferred_element_type=F32)
            r[here, cols] = total.astype(BF16)
            return 0

        lax.fori_loop(0, D // 512, tile, 0, unroll=True)
        if name == "A":
            y_top(2)
            ring_first("low1")
        elif name == "B":
            ring_first("low0")
        else:
            y_top({"1": 1, "2": -1, "3": 0}[name])

    def add(row, cols, source, first=0):
        lo, hi = cols[0], cols[0] + cols[1]

        def some(i, _):
            here = at(row + i * 16, 16)
            came = source()[at(i * 16, 16), first : first + cols[1]]
            r[here, lo:hi] = (r[here, lo:hi].astype(F32) + came.astype(F32)).astype(BF16)
            return 0

        lax.fori_loop(0, ROWS // 16, some, 0)

    def y_top(dx):
        i = ORDER.index(dx)
        back.put(i, part(r, lambda: me.block(dx, 1), TOP), lambda: yt.at[i], me.yn)

    def y_top_add(dx):
        i = ORDER.index(dx)
        back.got(i, lambda: yt.at[i])
        add(me.block(dx, 0), TOP, lambda: yt.at[i])
        if dx == 2:
            ring_first("top")

    ring_of = {
        "top": (0, TOP, TOP_A, TOP_B, 4, lambda: ta, lambda j: tc.at[j]),
        "low0": (0, LOW, LOW_A, LOW_B, 8, lambda: la.at[0], lambda j: lc.at[j]),
        "low1": (1, LOW, LOW_A, LOW_B, 12, lambda: la.at[1], lambda j: lc.at[2 + j]),
    }

    def ring_first(name):
        group_, _, a, b, i, halves, _ = ring_of[name]
        size = a[1]
        far = lambda: me.block(2, group_)
        back.put(i, part(r, far, a), lambda: halves().at[:, 0:size], me.xp)
        back.put(i + 1, part(r, far, b), lambda: halves().at[:, size : 2 * size], me.xm)

    def ring_second(name, j):
        group_, cols, a, b, i, halves, ends = ring_of[name]
        size = a[1]
        dx, half, to = ((1, a, me.xp), (-1, b, me.xm))[j]
        back.got(i + j, lambda: halves().at[:, j * size : j * size + size])
        add(me.block(dx, group_), half, halves, j * size)
        back.put(i + 2 + j, part(r, lambda: me.block(dx, group_), cols), lambda: ends(j), to)

    def ring_wait(name):
        _, _, _, _, i, _, ends = ring_of[name]
        back.got(i + 2, lambda: ends(0))
        back.got(i + 3, lambda: ends(1))

    def other_rows():
        ring_wait("low1")
        add(me.block(0, 1), LOW, lambda: lc.at[2])
        add(me.block(0, 1), LOW, lambda: lc.at[3])
        back.put(16, part(r, lambda: me.block(0, 1), LOW), whole(yl), me.yn)

    tasks["yl"] = other_rows
    for dx in (2, 1, -1):
        tasks["ya%d" % dx] = lambda dx=dx: y_top_add(dx)
    for name in ring_of:
        for j in range(2):
            tasks[name + "CD"[j]] = lambda name=name, j=j: ring_second(name, j)


    def grad_term(h, n, sibling):
        z = (me.z + ORDER[n]) % 4
        c = 1 - me.core if sibling else me.core
        return jnp.dot(kt[h], xg[:, at((z * 2 + c) * 512, 512)], preferred_element_type=F32)

    staged = (pbuf, sbuf)

    def near_put(h, n):
        staged[h][:, n * 512 : (n + 1) * 512] = grad_term(h, n, 1).astype(BF16)
        src = lambda: staged[h].at[:, n * 512 : (n + 1) * 512]
        near.put(h * 4 + n, src, lambda: gb.at[h * 4 + n], me.sib)

    def near_add(h, n):
        term = grad_term(h, n, 0)
        near.got(h * 4 + n, lambda: gb.at[h * 4 + n])
        gb[h * 4 + n] = (gb[h * 4 + n].astype(F32) + term).astype(BF16)
        if n == 0:
            lo, hi = slice(0, 256), slice(256, 512)
            rings.put(h * 6, lambda: gb.at[h * 4, lo], lambda: zb.at[h, lo], me.zp)
            rings.put(h * 6 + 1, lambda: gb.at[h * 4, hi], lambda: zb.at[h, hi], me.zm)

    def z_second(h, j):
        half = slice(j * 256, j * 256 + 256)
        chunk = h * 4 + 1 + j
        rings.got(h * 6 + j, lambda: zb.at[h, half])
        gb[chunk, half] = (gb[chunk, half].astype(F32) + zb[h, half].astype(F32)).astype(BF16)
        for i in range(2):
            here = slice(i * 256, i * 256 + 256)
            there = slice(512 * (1 + j) + i * 256, 512 * (1 + j) + i * 256 + 256)
            rings.put(
                h * 6 + 2 + 2 * j + i,
                lambda here=here: gb.at[chunk, here],
                lambda there=there: zb.at[h, there],
                (me.zp, me.zm)[j],
            )

    def z_sum(h, j):
        first, second = 512 + j * 256, 1024 + j * 256
        rings.got(h * 6 + 2 + j, lambda: zb.at[h, first : first + 256])
        rings.got(h * 6 + 4 + j, lambda: zb.at[h, second : second + 256])
        total = (
            gb[h * 4 + 3, j * 256 : j * 256 + 256].astype(F32)
            + zb[h, first : first + 256].astype(F32)
            + zb[h, second : second + 256].astype(F32)
        )
        if h == 0:
            col_grad[j * 256 : j * 256 + 256, :] = total
        else:
            ps[j] = total.astype(BF16)
            heads.put(17 + j, lambda: ps.at[j], lambda: pb.at[j], me.pair)

    def pair_sum(j):
        heads.got(17 + j, lambda: pb.at[j])
        col_grad[j * 256 : j * 256 + 256, :] += pb[j].astype(F32)

    for h in range(2):
        for n in range(4):
            tasks["np%d%d" % (h, n)] = lambda h=h, n=n: near_put(h, n)
            tasks["na%d%d" % (h, n)] = lambda h=h, n=n: near_add(h, n)
        for j in range(2):
            tasks["z%s%d" % ("CD"[j], h)] = lambda h=h, j=j: z_second(h, j)
            tasks["zs%d%d" % (h, j)] = lambda h=h, j=j: z_sum(h, j)
    for j in range(2):
        tasks["pf%d" % j] = lambda j=j: pair_sum(j)


    def finish():
        back.got(3, lambda: yt.at[3])
        ring_wait("low0")
        ring_wait("top")
        back.got(16, whole(yl))

        def total(cols, *sources):
            lo, hi = cols[0], cols[0] + cols[1]

            def some(i, _):
                grad = r[at(own + i * 16, 16), lo:hi].astype(F32)
                for source in sources:
                    grad += source()[at(i * 16, 16), :].astype(F32)
                row_grad[at(i * 16, 16), lo:hi] = grad.astype(BF16)
                return 0

            lax.fori_loop(0, ROWS // 16, some, 0)

        total(TOP, lambda: tc.at[0], lambda: tc.at[1], lambda: yt.at[3])
        total(LOW, lambda: lc.at[0], lambda: lc.at[1], whole(yl))
        heads.got(15, whole(att_out))
        heads.got(16, whole(dq_out))

    tasks["fin"] = finish

    for step in STEPS:
        name, _, only = step.partition("@")

        def run(name=name):
            if name in tasks:
                tasks[name]()
            elif name[0] == "o":
                project(name[1:], "o")
            elif name[0] == "g":
                project(name[2:], name[1])
            elif name == "kt0":
                turn(0)
            elif name == "kt1":
                for each in given:
                    got_grads(each)
                turn(1)
            else:
                row_terms({"RA": "A", "RB": "B", "R1": "1", "R-1": "2", "R0": "3"}[name])

        if only:
            pl.when(me.core == int(only))(run)
        else:
            run()

    for wires in (rows, weights, heads, back, near, rings):
        wires.close()


def results_kernel(enc, gain, row_grad, col_grad, att_in, dq_in, enc_grad, kg, vg, att, dq):
    wide = enc[...].astype(F32)
    factor = lax.rsqrt(jnp.mean(wide * wide, axis=-1, keepdims=True) + EPS)
    scaled = row_grad[...].astype(F32) * gain[...]
    inner = jnp.mean(scaled * wide, axis=-1, keepdims=True)
    enc_grad[...] = (factor * scaled - wide * (factor * factor * factor * inner)).astype(BF16)
    kg[...] = col_grad[0:HD, :].T
    vg[...] = col_grad[HD : 2 * HD, :].T
    att[...] = att_in[...]
    dq[...] = dq_in[...]


def on_device(enc_states, enc_gain, key_weight, value_weight, queries, out_grad, lengths):
    enc = enc_states[0]
    gain = enc_gain.reshape(1, D)
    vmem = pl.BlockSpec(memory_space=pltpu.VMEM)
    far = pl.BlockSpec(memory_space=pl.ANY)
    dma = pltpu.SemaphoreType.DMA
    shape = jax.ShapeDtypeStruct
    low = D - CUT

    row_grad, col_grad, att, dq = pl.pallas_call(
        kernel,
        out_shape=(
            shape((ROWS, D), BF16),
            shape((2 * HD, 512), F32),
            shape((TGT, HD), BF16),
            shape((TGT, HD), BF16),
        ),
        in_specs=[pl.BlockSpec(memory_space=pltpu.SMEM), vmem, vmem, far, far, far, far],
        out_specs=(vmem, vmem, far, far),
        scratch_shapes=[
            pltpu.VMEM((1024, D), BF16),
            pltpu.VMEM((D, 2 * HD), BF16),
            pltpu.VMEM((D, 2 * HD), BF16),
            pltpu.VMEM((2048, 2 * HD), BF16),
            pltpu.VMEM((1024, 2 * HD), BF16),
            pltpu.VMEM((TGT, HD), BF16),
            pltpu.VMEM((TGT, HD), BF16),
            pltpu.VMEM((TGT, 2048), BF16),
            pltpu.VMEM((TGT, 2048), BF16),
            pltpu.VMEM((TGT, HD), BF16),
            pltpu.VMEM((TGT, HD), BF16),
            pltpu.VMEM((2048, 2 * HD), BF16),
            pltpu.VMEM((1024, 2 * HD), BF16),
            pltpu.VMEM((2, 2 * HD, 1024), BF16),
            pltpu.VMEM((1024, D), BF16),
            pltpu.VMEM((4, ROWS, CUT), BF16),
            pltpu.VMEM((ROWS, CUT), BF16),
            pltpu.VMEM((2, ROWS, CUT), BF16),
            pltpu.VMEM((2, ROWS, low), BF16),
            pltpu.VMEM((4, ROWS, low), BF16),
            pltpu.VMEM((ROWS, low), BF16),
            pltpu.VMEM((8, 512, 512), BF16),
            pltpu.VMEM((2, 1536, 512), BF16),
            pltpu.VMEM((2, 256, 512), BF16),
            pltpu.VMEM((2, 256, 512), BF16),
            dma((17,)),
            dma((17,)),
            dma((20,)),
            dma((20,)),
            dma((19,)),
            dma((19,)),
            dma((17,)),
            dma((17,)),
            dma((8,)),
            dma((8,)),
            dma((12,)),
            dma((12,)),
            dma((2,)),
            pltpu.SemaphoreType.REGULAR((2,)),
        ],
        compiler_params=pltpu.CompilerParams(
            collective_id=0, has_side_effects=True, vmem_limit_bytes=VMEM_BYTES
        ),
        name="gather_attend_scatter",
    )(lengths, enc, gain, key_weight, value_weight, queries[0], out_grad[0])

    def rows_of(count, width):
        return pl.BlockSpec((count, width), lambda i: (i, 0))

    enc_grad, kg, vg, att, dq = pl.pallas_call(
        results_kernel,
        grid=(2,),
        out_shape=(
            shape((ROWS, D), BF16),
            shape((512, HD), F32),
            shape((512, HD), F32),
            shape((TGT, HD), BF16),
            shape((TGT, HD), BF16),
        ),
        in_specs=[
            rows_of(64, D),
            pl.BlockSpec((1, D), lambda i: (0, 0)),
            rows_of(64, D),
            pl.BlockSpec((2 * HD, 256), lambda i: (0, i)),
            rows_of(256, HD),
            rows_of(256, HD),
        ],
        out_specs=(
            rows_of(64, D),
            rows_of(256, HD),
            rows_of(256, HD),
            rows_of(256, HD),
            rows_of(256, HD),
        ),
        name="results",
    )(enc, gain, row_grad, col_grad, att, dq)
    return (att[None], enc_grad[None], kg, vg, dq[None])


def solution(mesh):
    placed = (
        P(("section", "dp"), "seq", None),
        P(),
        P(None, "seq"),
        P(None, "seq"),
        P(("section", "dp"), None, "seq"),
        P(("section", "dp"), None, "seq"),
        P(),
    )
    return jax.shard_map(
        on_device,
        mesh=mesh,
        in_specs=placed,
        out_specs=(
            P(("section", "dp"), None, "seq"),
            P(("section", "dp"), "seq", None),
            P(("section", "dp"), "seq"),
            P(("section", "dp"), "seq"),
            P(("section", "dp"), None, "seq"),
        ),
        check_vma=False,
    )
```

time: 147 us -> 140 us (0.952)
  Pallas kernels: 146 us -> 139 us
    pallas_call x1, Pallas kernels: 141 us -> 136 us  [on_device(): pl.pallas_call(kernel, out_shape=(shape((ROWS, D), BF16), shape((2 * HD,...]
where the time goes in v3:
time: 140 us
  Pallas kernels  139 us (99%)
    pallas_call x1, Pallas kernels, on_device(): pl.pallas_call(kernel, out_shape=(shape((ROWS, D), BF16), shape((2 * HD,...  136 us
    pallas_call x1, Pallas kernels, on_device(): pl.pallas_call(results_kernel, grid=(2,), out_shape=(shape((ROWS, D), BF1...  3.87 us

profile of v3, /device:TPU:1, one launch (start us, length us, event | category | flops | bytes accessed | tf_op | source)
XLA Modules:
  0.0 140.2 jit_solution(6219864342062661470)
XLA Ops:
  0.6 135.5 %gather_attend_scatter.1 = (bf16[128,4096]{1,0:T(8,128)(2,1)}, f32[512,512]{1,0:T(8,128)}, bf16[512,256]{1,0:T(8,128)(2,1)}, bf16[512,256]{1,0:T(8,128)(2,1)}) custom-call(s32[8]{0:T(128)} %len_ref.1, bf16[128,4096]{1,0:T(8,128)(2,1)} %bitcast.7, f32[1,4096]{1,0:T(1,128)} %bitcast.11, bf16[4096,256]{1,0:T(8,128)(2,1)} %kw.1, bf16[4096,256]{1,0:T(8,128)(2,1)} %vw.1, ...), custom_call_target="tpu_custom_call" | custom-call | tf_op jit(solution)/shard_map/gather_attend_scatter/pallas_call | solution.py:655
  136.1 3.9 %results.1 = (bf16[128,4096]{1,0:T(8,128)(2,1)}, f32[512,256]{1,0:T(8,128)}, f32[512,256]{1,0:T(8,128)}, bf16[512,256]{1,0:T(8,128)(2,1)}, bf16[512,256]{1,0:T(8,128)(2,1)}) custom-call(bf16[128,4096]{1,0:T(8,128)(2,1)} %bitcast.8, f32[1,4096]{1,0:T(1,128)} %bitcast.12, bf16[128,4096]{1,0:T(8,128)(2,1)} %get-tuple-element.14.row_grad, ...), custom_call_target="tpu_custom_call" | custom-call | tf_op jit(solution)/shard_map/results/pallas_call | solution.py:715

commit v4 on v3

--- a/solution.py
+++ b/solution.py
@@ -94,8 +94,9 @@
     def got(self, i, dst):
         self.copy(i, dst(), dst(), self.home).wait_recv()
 
-    def close(self):
-        for i, src in self.open.items():
+    def close(self, ids=None):
+        for i in list(self.open) if ids is None else ids:
+            src = self.open.pop(i)
             self.copy(i, src(), src(), self.home).wait_send()
 
 
@@ -140,15 +141,15 @@
 ORDER = (2, 1, -1, 0)
 STEPS = (
     "begin@0", "r1@0", "r8@0", "w1K", "w1V", "r0@0", "r10@0", "r9@0", "r13@0", "r23@0", "w2aK",
-    "r14@0", "w2bK", "gate@0", "w2aV", "w2bV", "begin@1", "w3K", "w3V", "wallK", "r8@1",
-    "wallV", "r0@1", "r1@1", "q", "gV0", "r9@1", "gK0", "o0", "r13@1", "r10@1", "gV-1", "r23@1",
-    "r14@1", "gK-1", "gV1", "o1", "gK1", "gate3@1", "gVfar", "ofar", "g", "gVlast", "gKlast",
-    "gKfar", "o-1", "olast", "att", "ao", "hgpA", "hgo1", "hgo0", "hgo3", "hgo2", "hgpB",
-    "hgp1", "hgp2", "kt0", "hgp3", "np00", "na00@1", "na02@1", "RA", "na01@1", "np02", "RB",
-    "zD0@1", "np01", "zC0@1", "R1", "low1C", "R-1", "low1D", "na00@0", "kt1", "np10", "np11",
-    "ya2", "R0", "na02@0", "na01@0", "np12", "zD0@0", "zC0@0", "low0D", "low0C", "np03", "ya1",
-    "np13", "na10", "yl", "na11", "na12", "na03", "ya-1", "topC", "zs00", "zD1", "zC1", "na13",
-    "topD", "zs10", "zs11", "zs01", "pf0", "fin", "pf1",
+    "r14@0", "w2bK", "gate@0", "w2aV", "w2bV", "begin@1", "gate3@1", "w3K", "w3V", "wallK",
+    "r8@1", "wallV", "r0@1", "r1@1", "q", "gV0", "r9@1", "gK0", "o0", "r13@1", "r10@1", "gV-1",
+    "r23@1", "r14@1", "gK-1", "gV1", "o1", "gK1", "gVfar", "ofar", "g", "gVlast", "gKlast",
+    "gKfar", "o-1", "olast", "att", "hgpA", "hgo1", "hgo0", "hgo3", "hgo2", "hgpB", "hgp1",
+    "hgp2", "kt0", "hgp3", "ao@0", "ad@0", "np00", "na00@1", "na02@1", "RA", "na01@1", "np02",
+    "RB", "zD0@1", "np01", "zC0@1", "R1", "low1C", "R-1", "low1D", "na00@0", "kt1", "np10",
+    "np11", "ya2", "R0", "na02@0", "na01@0", "np12", "zD0@0", "zC0@0", "low0D", "low0C", "np03",
+    "ya1", "np13", "na10", "yl", "na11", "na12", "na03", "ya-1", "topC", "zs00", "zD1", "zC1",
+    "ao@1", "ad@1", "na13", "topD", "zs10", "zs11", "zs01", "pf0", "fin", "pf1",
 )
 
 
@@ -156,7 +157,7 @@
     len_ref, enc, gain, kw, vw, q, g,
     row_grad, col_grad, att_out, dq_out,
     xg, w, wp, kv, kvs, qr, gr, pbuf, sbuf, att, dq, kvg, kvp, kt,
-    r, yt, ta, tc, la, lc, yl, gb, zb, ps, pb,
+    r, yt, ta, tc, la, lc, yl, gb, zb, ps, pb, rg, cg,
     xs, xr, ws, wr, hs, hr, bs, br, ns, nr, zs, zr, loc, gates,
 ):
     me = Place()
@@ -413,11 +414,8 @@
     for i, dx in enumerate(ORDER):
         tasks["hgo%d" % i] = lambda dx=dx: head_grads(me.column(dx), 256)
 
-    def results_back():
-        heads.put(15, whole(att), whole(att_out), me.across)
-        heads.put(16, whole(dq), whole(dq_out), me.across)
-
-    tasks["ao"] = results_back
+    tasks["ao"] = lambda: heads.put(15, whole(att), whole(att_out), me.across)
+    tasks["ad"] = lambda: heads.put(16, whole(dq), whole(dq_out), me.across)
 
     def turn(h):
         kt[h] = (kvg[0:1024, :] if h == 0 else kvp[...]).T
@@ -558,14 +556,24 @@
             + zb[h, second : second + 256].astype(F32)
         )
         if h == 0:
-            col_grad[j * 256 : j * 256 + 256, :] = total
+            cg[j * 256 : j * 256 + 256, :] = total
         else:
             ps[j] = total.astype(BF16)
             heads.put(17 + j, lambda: ps.at[j], lambda: pb.at[j], me.pair)
 
+    def col_out(j):
+        half = slice(j * 256, j * 256 + 256)
+        return pltpu.make_async_copy(cg.at[half], col_grad.at[half], loc.at[2 + j])
+
+    def row_out(j):
+        lo, size = (TOP, LOW)[j]
+        part_ = slice(lo, lo + size)
+        return pltpu.make_async_copy(rg.at[:, part_], row_grad.at[:, part_], loc.at[4 + j])
+
     def pair_sum(j):
         heads.got(17 + j, lambda: pb.at[j])
-        col_grad[j * 256 : j * 256 + 256, :] += pb[j].astype(F32)
+        cg[j * 256 : j * 256 + 256, :] += pb[j].astype(F32)
+        col_out(j).start()
 
     for h in range(2):
         for n in range(4):
@@ -579,10 +587,15 @@
 
 
     def finish():
+        rows.close()
+        weights.close()
+        near.close()
+        heads.close(range(15))
+        back.close((0, 1, 2, 3, 4, 5, 8, 9, 12, 13))
+        rings.close((0, 1, 2, 3, 4, 5, 6, 7))
         back.got(3, lambda: yt.at[3])
         ring_wait("low0")
         ring_wait("top")
-        back.got(16, whole(yl))
 
         def total(cols, *sources):
             lo, hi = cols[0], cols[0] + cols[1]
@@ -591,13 +604,16 @@
                 grad = r[at(own + i * 16, 16), lo:hi].astype(F32)
                 for source in sources:
                     grad += source()[at(i * 16, 16), :].astype(F32)
-                row_grad[at(i * 16, 16), lo:hi] = grad.astype(BF16)
+                rg[at(i * 16, 16), lo:hi] = grad.astype(BF16)
                 return 0
 
             lax.fori_loop(0, ROWS // 16, some, 0)
 
         total(TOP, lambda: tc.at[0], lambda: tc.at[1], lambda: yt.at[3])
+        row_out(0).start()
+        back.got(16, whole(yl))
         total(LOW, lambda: lc.at[0], lambda: lc.at[1], whole(yl))
+        row_out(1).start()
         heads.got(15, whole(att_out))
         heads.got(16, whole(dq_out))
 
@@ -629,6 +645,9 @@
 
     for wires in (rows, weights, heads, back, near, rings):
         wires.close()
+    for j in range(2):
+        col_out(j).wait()
+        row_out(j).wait()
 
 
 def results_kernel(enc, gain, row_grad, col_grad, att_in, dq_in, enc_grad, kg, vg, att, dq):
@@ -661,7 +680,7 @@
             shape((TGT, HD), BF16),
         ),
         in_specs=[pl.BlockSpec(memory_space=pltpu.SMEM), vmem, vmem, far, far, far, far],
-        out_specs=(vmem, vmem, far, far),
+        out_specs=(far, far, far, far),
         scratch_shapes=[
             pltpu.VMEM((1024, D), BF16),
             pltpu.VMEM((D, 2 * HD), BF16),
@@ -688,6 +707,8 @@
             pltpu.VMEM((2, 1536, 512), BF16),
             pltpu.VMEM((2, 256, 512), BF16),
             pltpu.VMEM((2, 256, 512), BF16),
+            pltpu.VMEM((ROWS, D), BF16),
+            pltpu.VMEM((2 * HD, 512), F32),
             dma((17,)),
             dma((17,)),
             dma((20,)),
@@ -700,7 +721,7 @@
             dma((8,)),
             dma((12,)),
             dma((12,)),
-            dma((2,)),
+            dma((6,)),
             pltpu.SemaphoreType.REGULAR((2,)),
         ],
         compiler_params=pltpu.CompilerParams(

time: 140 us -> 139 us (level)
  the two profiles are of different devices: /device:TPU:1 before, /device:TPU:3 now
where the time goes in v4:
time: 139 us
  Pallas kernels  138 us (99%)
    pallas_call x1, Pallas kernels, on_device(): pl.pallas_call(kernel, out_shape=(shape((ROWS, D), BF16), shape((2 * HD,...  134 us
    pallas_call x1, Pallas kernels, on_device(): pl.pallas_call(results_kernel, grid=(2,), out_shape=(shape((ROWS, D), BF1...  3.87 us

profile of v4, /device:TPU:3, one launch (start us, length us, event | category | flops | bytes accessed | tf_op | source)
XLA Modules:
  0.0 139.0 jit_solution(3313439821838722288)
XLA Ops:
  0.6 134.3 %gather_attend_scatter.1 = (bf16[128,4096]{1,0:T(8,128)(2,1)}, f32[512,512]{1,0:T(8,128)}, bf16[512,256]{1,0:T(8,128)(2,1)}, bf16[512,256]{1,0:T(8,128)(2,1)}) custom-call(s32[8]{0:T(128)} %len_ref.1, bf16[128,4096]{1,0:T(8,128)(2,1)} %bitcast.7, f32[1,4096]{1,0:T(1,128)} %bitcast.11, bf16[4096,256]{1,0:T(8,128)(2,1)} %kw.1, bf16[4096,256]{1,0:T(8,128)(2,1)} %vw.1, ...), custom_call_target="tpu_custom_call" | custom-call | tf_op jit(solution)/shard_map/gather_attend_scatter/pallas_call | solution.py:674
  134.9 3.9 %results.1 = (bf16[128,4096]{1,0:T(8,128)(2,1)}, f32[512,256]{1,0:T(8,128)}, f32[512,256]{1,0:T(8,128)}, bf16[512,256]{1,0:T(8,128)(2,1)}, bf16[512,256]{1,0:T(8,128)(2,1)}) custom-call(bf16[128,4096]{1,0:T(8,128)(2,1)} %bitcast.8, f32[1,4096]{1,0:T(1,128)} %bitcast.12, bf16[128,4096]{1,0:T(8,128)(2,1)} %get-tuple-element.14.row_grad, ...), custom_call_target="tpu_custom_call" | custom-call | tf_op jit(solution)/shard_map/results/pallas_call | solution.py:736
